TPU v7x, 32 devices: a whole 2x2x4 slice. The times are simulated.
32 devices in a mesh: tm: 4 (over y, x), space: 8 (over z, core).
Axes of the slice: x: 2, y: 2, z: 4, core: 2. Of those that a mesh axis runs over, the one named last changes fastest.
Arguments:
- source: float32 [64, 3, 32, 8, 128], P('tm', None, 'space'), may hold values from -24 to 24
- coarse_start: float32 [4, 3, 32, 8, 128], P('tm', None, 'space'), may hold values from -6 to 6
- region: int32 [32, 8, 128], P('space'), may hold values from 0 to 7
- reluctivity: float32 [8], replicated, may hold values from 0.25 to 2
- conductance: float32 [8], replicated, may hold values from 0.25 to 4
Outputs:
- states: float32 [64, 3, 32, 8, 128], P('tm', None, 'space')
All inputs are finite; a program needn't handle non-finite values.
Results may differ from a plain program's by a relative error of at most 0.00002.
Values sent between devices are 32-bit elements; how exact they have to be, the bound alone decides.
A program may use at most 64 MiB of HBM per device.

v0:
```python
import jax
import jax.numpy as jnp
from jax import lax
from jax.sharding import PartitionSpec as P

FINE = 16
SWEEPS = 4


lamination_ratio = 8.0


def with_halo(block, sides, width):
    for axis, dim in sides:
        count = lax.axis_size(axis)
        forward = [(i, i + 1) for i in range(count - 1)]
        backward = [(target, source) for source, target in forward]
        low = lax.ppermute(
            lax.slice_in_dim(block, block.shape[dim] - width, None, axis=dim), axis, forward
        )
        high = lax.ppermute(lax.slice_in_dim(block, 0, width, axis=dim), axis, backward)
        block = jnp.concatenate([low, block, high], axis=dim)
    return block


def passed_along(block, axis, distance):
    devices = range(lax.axis_size(axis))
    route = [((i - distance) % len(devices), i) for i in devices]
    return lax.ppermute(block, axis, route)


def lookup(region, values_table):
    levels = jnp.arange(values_table.shape[0], dtype=jnp.int32)
    matches = (region[None] == levels[:, None, None, None]).astype(values_table.dtype)
    return jnp.sum(matches * values_table[:, None, None, None], axis=0)


def face_terms(reluct):
    padded = jnp.pad(reluct, ((1, 1), (0, 0), (0, 0)))
    faces_z = 0.5 * lamination_ratio * (padded[1:] + padded[:-1])
    padded = jnp.pad(reluct, ((0, 0), (1, 1), (0, 0)))
    faces_x = 0.5 * (padded[:, 1:] + padded[:, :-1])
    padded = jnp.pad(reluct, ((0, 0), (0, 0), (1, 1)))
    faces_y = 0.5 * (padded[:, :, 1:] + padded[:, :, :-1])
    summed = (
        faces_z[1:]
        + faces_z[:-1]
        + faces_x[:, 1:]
        + faces_x[:, :-1]
        + faces_y[:, :, 1:]
        + faces_y[:, :, :-1]
    )
    return (faces_z, faces_x, faces_y, summed)


def couple(field, faces_z, faces_x, faces_y):
    padded = jnp.pad(field, ((0, 0), (1, 1), (0, 0), (0, 0)))
    result = faces_z[1:] * padded[:, 2:] + faces_z[:-1] * padded[:, :-2]
    padded = jnp.pad(field, ((0, 0), (0, 0), (1, 1), (0, 0)))
    result = result + faces_x[:, 1:] * padded[:, :, 2:] + faces_x[:, :-1] * padded[:, :, :-2]
    padded = jnp.pad(field, ((0, 0), (0, 0), (0, 0), (1, 1)))
    result = (
        result + faces_y[:, :, 1:] * padded[:, :, :, 2:] + faces_y[:, :, :-1] * padded[:, :, :, :-2]
    )
    return result


def local(source, coarse_start, region, reluctivity, conductance):
    planes = source.shape[2]
    slabs = lax.axis_size("space")
    reluct = lookup(region, reluctivity)
    conduct = lookup(region, conductance)
    rimmed = with_halo(jnp.stack([conduct, reluct]), (("space", 1),), SWEEPS)
    conduct_rim = rimmed[0]
    reluct_rim = rimmed[1]
    global_plane = (
        lax.axis_index("space") * planes - SWEEPS + jnp.arange(planes + 2 * SWEEPS, dtype=jnp.int32)
    )
    inside = ((global_plane >= 0) & (global_plane < planes * slabs)).astype(jnp.float32)[
        :, None, None
    ]
    outside = 1.0 - inside
    faces_z, faces_x, faces_y, summed = face_terms(reluct_rim)
    fine_divisor = conduct_rim + summed + outside
    coarse_divisor = conduct_rim / FINE + summed + outside

    def sweeps(field, driving, divisor):
        for sweep_index in range(SWEEPS):
            field = (driving + couple(field, faces_z, faces_x, faces_y)) / divisor * inside
        return field[:, SWEEPS : SWEEPS + planes]

    def advance(state, plain_source):
        stacked = with_halo(jnp.stack([state, plain_source]), (("space", 2),), SWEEPS)
        field = stacked[0]
        forcing = stacked[1]
        return sweeps(field, conduct_rim * field + forcing, fine_divisor)

    start_state = coarse_start[0]

    def relax_step(field, paired):
        result = advance(field, paired[0])
        return (result, result)

    final_state, later_states = lax.scan(relax_step, start_state, (source[1:], source[1:]))
    states = jnp.concatenate([start_state[None], later_states], axis=0)
    arrived = passed_along(final_state, "tm", 1)
    arrived = advance(arrived, source[0])
    residual = arrived - states[0]
    my_turn = lax.axis_index("tm")

    def coarse_turn(turn_index, carried):
        previous, kept_value = carried
        incoming = passed_along(previous, "tm", 1)
        field = with_halo(incoming, (("space", 1),), SWEEPS)
        update = sweeps(field, conduct_rim / FINE * field, coarse_divisor) + residual
        kept_value = jnp.where(my_turn == turn_index, update, kept_value)
        return (update, kept_value)

    final_pair = lax.fori_loop(
        0, lax.axis_size("tm"), coarse_turn, (residual, jnp.zeros_like(residual))
    )
    correction = final_pair[1]
    return states.at[0].add(correction)


def solution(mesh):
    placed = (
        P("tm", None, "space", None, None),
        P("tm", None, "space", None, None),
        P("space", None, None),
        P(),
        P(),
    )
    return jax.shard_map(
        local,
        mesh=mesh,
        in_specs=placed,
        out_specs=P("tm", None, "space", None, None),
        check_vma=False,
    )
```

profile of v0, /device:TPU:1, one launch (start us, length us, event | category | flops | bytes accessed | tf_op | source)
XLA Modules:
  0.0 210.7 jit_solution(963836078803643578)
XLA Ops:
  0.8 4.7 %collective-permute-start.5 = (f32[2,4,8,128]{3,2,1,0:T(8,128)S(1)}, f32[2,4,8,128]{3,2,1,0:T(8,128)S(1)}, u32[]{:S(2)}, u32[]{:S(2)}) collective-permute-start(f32[2,4,8,128]{3,2,1,0:T(8,128)S(1)} %pad_maximum_fusion.6), channel_id=1, source_target_pairs={{0,1},{1,2},{2,3},{3,4},{4,5},{5,6},{6,7},{8,9},{9,10},{10,11},{11... | collective-permute-start | bytes 98312 | tf_op jit(solution)/shard_map/ppermute | solution.py:18
  11.9 129.5 %while.34 = (s32[]{:T(128)}, f32[3,4,8,128]{3,2,1,0:T(8,128)S(1)}, f32[15,3,4,8,128]{4,3,2,1,0:T(8,128)S(1)}, f32[1,12,8,128]{3,2,1,0:T(8,128)S(1)}, f32[15,3,4,...) while((s32[]{:T(128)}, f32[3,4,8,128]{3,2,1,0:T(8,128)S(1)}, ...), condition=%wide.region_3.4_spmd.clone, body=%wide.region_2.3_spmd.clone.sunk | while | flops 2187326 | bytes 6685617 | solution.py:104
  13.9 3.6 %collective-permute-start.1 = (f32[2,3,4,8,128]{4,3,2,1,0:T(8,128)S(1)}, f32[2,3,4,8,128]{4,3,2,1,0:T(8,128)S(1)}, u32[]{:S(2)}, u32[]{:S(2)}) collective-permute-start(f32[2,3,4,8,128]{4,3,2,1,0:T(8,128)S(1)} %pad_maximum_fusion.9), channel_id=1, source_target_pairs={{0,1},{1,2},{2,3},{3,4},{4,5},{5,6},{6,7},{8,9},{9,10},{10,11},{11... | collective-permute-start | bytes 294920 | tf_op jit(solution)/shard_map/while/body/eval_jaxpr/ppermute | solution.py:18
  21.9 4.3 %collective-permute-start.1 = (f32[2,3,4,8,128]{4,3,2,1,0:T(8,128)S(1)}, f32[2,3,4,8,128]{4,3,2,1,0:T(8,128)S(1)}, u32[]{:S(2)}, u32[]{:S(2)}) collective-permute-start(f32[2,3,4,8,128]{4,3,2,1,0:T(8,128)S(1)} %pad_maximum_fusion.9), channel_id=1, source_target_pairs={{0,1},{1,2},{2,3},{3,4},{4,5},{5,6},{6,7},{8,9},{9,10},{10,11},{11... | collective-permute-start | bytes 294920 | tf_op jit(solution)/shard_map/while/body/eval_jaxpr/ppermute | solution.py:18
  30.6 4.3 %collective-permute-start.1 = (f32[2,3,4,8,128]{4,3,2,1,0:T(8,128)S(1)}, f32[2,3,4,8,128]{4,3,2,1,0:T(8,128)S(1)}, u32[]{:S(2)}, u32[]{:S(2)}) collective-permute-start(f32[2,3,4,8,128]{4,3,2,1,0:T(8,128)S(1)} %pad_maximum_fusion.9), channel_id=1, source_target_pairs={{0,1},{1,2},{2,3},{3,4},{4,5},{5,6},{6,7},{8,9},{9,10},{10,11},{11... | collective-permute-start | bytes 294920 | tf_op jit(solution)/shard_map/while/body/eval_jaxpr/ppermute | solution.py:18
  39.2 4.3 %collective-permute-start.1 = (f32[2,3,4,8,128]{4,3,2,1,0:T(8,128)S(1)}, f32[2,3,4,8,128]{4,3,2,1,0:T(8,128)S(1)}, u32[]{:S(2)}, u32[]{:S(2)}) collective-permute-start(f32[2,3,4,8,128]{4,3,2,1,0:T(8,128)S(1)} %pad_maximum_fusion.9), channel_id=1, source_target_pairs={{0,1},{1,2},{2,3},{3,4},{4,5},{5,6},{6,7},{8,9},{9,10},{10,11},{11... | collective-permute-start | bytes 294920 | tf_op jit(solution)/shard_map/while/body/eval_jaxpr/ppermute | solution.py:18
  47.9 4.3 %collective-permute-start.1 = (f32[2,3,4,8,128]{4,3,2,1,0:T(8,128)S(1)}, f32[2,3,4,8,128]{4,3,2,1,0:T(8,128)S(1)}, u32[]{:S(2)}, u32[]{:S(2)}) collective-permute-start(f32[2,3,4,8,128]{4,3,2,1,0:T(8,128)S(1)} %pad_maximum_fusion.9), channel_id=1, source_target_pairs={{0,1},{1,2},{2,3},{3,4},{4,5},{5,6},{6,7},{8,9},{9,10},{10,11},{11... | collective-permute-start | bytes 294920 | tf_op jit(solution)/shard_map/while/body/eval_jaxpr/ppermute | solution.py:18
  56.6 4.3 %collective-permute-start.1 = (f32[2,3,4,8,128]{4,3,2,1,0:T(8,128)S(1)}, f32[2,3,4,8,128]{4,3,2,1,0:T(8,128)S(1)}, u32[]{:S(2)}, u32[]{:S(2)}) collective-permute-start(f32[2,3,4,8,128]{4,3,2,1,0:T(8,128)S(1)} %pad_maximum_fusion.9), channel_id=1, source_target_pairs={{0,1},{1,2},{2,3},{3,4},{4,5},{5,6},{6,7},{8,9},{9,10},{10,11},{11... | collective-permute-start | bytes 294920 | tf_op jit(solution)/shard_map/while/body/eval_jaxpr/ppermute | solution.py:18
  65.3 4.3 %collective-permute-start.1 = (f32[2,3,4,8,128]{4,3,2,1,0:T(8,128)S(1)}, f32[2,3,4,8,128]{4,3,2,1,0:T(8,128)S(1)}, u32[]{:S(2)}, u32[]{:S(2)}) collective-permute-start(f32[2,3,4,8,128]{4,3,2,1,0:T(8,128)S(1)} %pad_maximum_fusion.9), channel_id=1, source_target_pairs={{0,1},{1,2},{2,3},{3,4},{4,5},{5,6},{6,7},{8,9},{9,10},{10,11},{11... | collective-permute-start | bytes 294920 | tf_op jit(solution)/shard_map/while/body/eval_jaxpr/ppermute | solution.py:18
  73.9 4.3 %collective-permute-start.1 = (f32[2,3,4,8,128]{4,3,2,1,0:T(8,128)S(1)}, f32[2,3,4,8,128]{4,3,2,1,0:T(8,128)S(1)}, u32[]{:S(2)}, u32[]{:S(2)}) collective-permute-start(f32[2,3,4,8,128]{4,3,2,1,0:T(8,128)S(1)} %pad_maximum_fusion.9), channel_id=1, source_target_pairs={{0,1},{1,2},{2,3},{3,4},{4,5},{5,6},{6,7},{8,9},{9,10},{10,11},{11... | collective-permute-start | bytes 294920 | tf_op jit(solution)/shard_map/while/body/eval_jaxpr/ppermute | solution.py:18
  82.6 4.3 %collective-permute-start.1 = (f32[2,3,4,8,128]{4,3,2,1,0:T(8,128)S(1)}, f32[2,3,4,8,128]{4,3,2,1,0:T(8,128)S(1)}, u32[]{:S(2)}, u32[]{:S(2)}) collective-permute-start(f32[2,3,4,8,128]{4,3,2,1,0:T(8,128)S(1)} %pad_maximum_fusion.9), channel_id=1, source_target_pairs={{0,1},{1,2},{2,3},{3,4},{4,5},{5,6},{6,7},{8,9},{9,10},{10,11},{11... | collective-permute-start | bytes 294920 | tf_op jit(solution)/shard_map/while/body/eval_jaxpr/ppermute | solution.py:18
  91.3 4.3 %collective-permute-start.1 = (f32[2,3,4,8,128]{4,3,2,1,0:T(8,128)S(1)}, f32[2,3,4,8,128]{4,3,2,1,0:T(8,128)S(1)}, u32[]{:S(2)}, u32[]{:S(2)}) collective-permute-start(f32[2,3,4,8,128]{4,3,2,1,0:T(8,128)S(1)} %pad_maximum_fusion.9), channel_id=1, source_target_pairs={{0,1},{1,2},{2,3},{3,4},{4,5},{5,6},{6,7},{8,9},{9,10},{10,11},{11... | collective-permute-start | bytes 294920 | tf_op jit(solution)/shard_map/while/body/eval_jaxpr/ppermute | solution.py:18
  100.0 4.3 %collective-permute-start.1 = (f32[2,3,4,8,128]{4,3,2,1,0:T(8,128)S(1)}, f32[2,3,4,8,128]{4,3,2,1,0:T(8,128)S(1)}, u32[]{:S(2)}, u32[]{:S(2)}) collective-permute-start(f32[2,3,4,8,128]{4,3,2,1,0:T(8,128)S(1)} %pad_maximum_fusion.9), channel_id=1, source_target_pairs={{0,1},{1,2},{2,3},{3,4},{4,5},{5,6},{6,7},{8,9},{9,10},{10,11},{11... | collective-permute-start | bytes 294920 | tf_op jit(solution)/shard_map/while/body/eval_jaxpr/ppermute | solution.py:18
  108.7 4.3 %collective-permute-start.1 = (f32[2,3,4,8,128]{4,3,2,1,0:T(8,128)S(1)}, f32[2,3,4,8,128]{4,3,2,1,0:T(8,128)S(1)}, u32[]{:S(2)}, u32[]{:S(2)}) collective-permute-start(f32[2,3,4,8,128]{4,3,2,1,0:T(8,128)S(1)} %pad_maximum_fusion.9), channel_id=1, source_target_pairs={{0,1},{1,2},{2,3},{3,4},{4,5},{5,6},{6,7},{8,9},{9,10},{10,11},{11... | collective-permute-start | bytes 294920 | tf_op jit(solution)/shard_map/while/body/eval_jaxpr/ppermute | solution.py:18
  117.3 4.3 %collective-permute-start.1 = (f32[2,3,4,8,128]{4,3,2,1,0:T(8,128)S(1)}, f32[2,3,4,8,128]{4,3,2,1,0:T(8,128)S(1)}, u32[]{:S(2)}, u32[]{:S(2)}) collective-permute-start(f32[2,3,4,8,128]{4,3,2,1,0:T(8,128)S(1)} %pad_maximum_fusion.9), channel_id=1, source_target_pairs={{0,1},{1,2},{2,3},{3,4},{4,5},{5,6},{6,7},{8,9},{9,10},{10,11},{11... | collective-permute-start | bytes 294920 | tf_op jit(solution)/shard_map/while/body/eval_jaxpr/ppermute | solution.py:18
  126.0 4.3 %collective-permute-start.1 = (f32[2,3,4,8,128]{4,3,2,1,0:T(8,128)S(1)}, f32[2,3,4,8,128]{4,3,2,1,0:T(8,128)S(1)}, u32[]{:S(2)}, u32[]{:S(2)}) collective-permute-start(f32[2,3,4,8,128]{4,3,2,1,0:T(8,128)S(1)} %pad_maximum_fusion.9), channel_id=1, source_target_pairs={{0,1},{1,2},{2,3},{3,4},{4,5},{5,6},{6,7},{8,9},{9,10},{10,11},{11... | collective-permute-start | bytes 294920 | tf_op jit(solution)/shard_map/while/body/eval_jaxpr/ppermute | solution.py:18
  134.7 4.3 %collective-permute-start.1 = (f32[2,3,4,8,128]{4,3,2,1,0:T(8,128)S(1)}, f32[2,3,4,8,128]{4,3,2,1,0:T(8,128)S(1)}, u32[]{:S(2)}, u32[]{:S(2)}) collective-permute-start(f32[2,3,4,8,128]{4,3,2,1,0:T(8,128)S(1)} %pad_maximum_fusion.9), channel_id=1, source_target_pairs={{0,1},{1,2},{2,3},{3,4},{4,5},{5,6},{6,7},{8,9},{9,10},{10,11},{11... | collective-permute-start | bytes 294920 | tf_op jit(solution)/shard_map/while/body/eval_jaxpr/ppermute | solution.py:18
  145.3 5.5 %collective-permute-start.8 = (f32[2,3,4,8,128]{4,3,2,1,0:T(8,128)S(1)}, f32[2,3,4,8,128]{4,3,2,1,0:T(8,128)S(1)}, u32[]{:S(2)}, u32[]{:S(2)}) collective-permute-start(f32[2,3,4,8,128]{4,3,2,1,0:T(8,128)S(1)} %pad_maximum_fusion.5), channel_id=1, source_target_pairs={{0,1},{1,2},{2,3},{3,4},{4,5},{5,6},{6,7},{8,9},{9,10},{10,11},{11... | collective-permute-start | bytes 294920 | tf_op jit(solution)/shard_map/ppermute | solution.py:18
  157.5 52.6 %while.35 = (s32[]{:T(128)}, f32[3,4,8,128]{3,2,1,0:T(8,128)S(1)}, f32[3,4,8,128]{3,2,1,0:T(8,128)S(1)}, f32[12,8,128]{2,1,0:T(8,128)S(1)}, f32[13,8,128]{2,1,0:...) while((s32[]{:T(128)}, f32[3,4,8,128]{3,2,1,0:T(8,128)S(1)}, ...), condition=%wide.region_5.6_spmd.clone, body=%wide.region_4.5_spmd.clone.sunk | while | flops 1953856 | bytes 5505533 | solution.py:119
  166.4 3.4 %collective-permute-done.4 = f32[3,4,8,128]{3,2,1,0:T(8,128)S(1)} collective-permute-done((f32[3,4,8,128]{3,2,1,0:T(8,128)S(1)}, f32[3,4,8,128]{3,2,1,0:T(8,128)S(1)}, u32[]{:S(2)}, u32[]{:S(2)}) %collective-permute-start.4) | collective-permute-done | bytes 49184 | tf_op jit(solution)/shard_map/while/body/eval_jaxpr/ppermute | solution.py:21
  170.8 3.7 %collective-permute-done.2 = f32[3,4,8,128]{3,2,1,0:T(8,128)S(1)} collective-permute-done((f32[3,4,8,128]{3,2,1,0:T(8,128)S(1)}, f32[3,4,8,128]{3,2,1,0:T(8,128)S(1)}, u32[]{:S(2)}, u32[]{:S(2)}) %collective-permute-start.2) | collective-permute-done | bytes 49184 | tf_op jit(solution)/shard_map/while/body/eval_jaxpr/ppermute | solution.py:29
  179.6 3.4 %collective-permute-done.4 = f32[3,4,8,128]{3,2,1,0:T(8,128)S(1)} collective-permute-done((f32[3,4,8,128]{3,2,1,0:T(8,128)S(1)}, f32[3,4,8,128]{3,2,1,0:T(8,128)S(1)}, u32[]{:S(2)}, u32[]{:S(2)}) %collective-permute-start.4) | collective-permute-done | bytes 49184 | tf_op jit(solution)/shard_map/while/body/eval_jaxpr/ppermute | solution.py:21
  184.0 3.7 %collective-permute-done.2 = f32[3,4,8,128]{3,2,1,0:T(8,128)S(1)} collective-permute-done((f32[3,4,8,128]{3,2,1,0:T(8,128)S(1)}, f32[3,4,8,128]{3,2,1,0:T(8,128)S(1)}, u32[]{:S(2)}, u32[]{:S(2)}) %collective-permute-start.2) | collective-permute-done | bytes 49184 | tf_op jit(solution)/shard_map/while/body/eval_jaxpr/ppermute | solution.py:29
  197.1 3.7 %collective-permute-done.2 = f32[3,4,8,128]{3,2,1,0:T(8,128)S(1)} collective-permute-done((f32[3,4,8,128]{3,2,1,0:T(8,128)S(1)}, f32[3,4,8,128]{3,2,1,0:T(8,128)S(1)}, u32[]{:S(2)}, u32[]{:S(2)}) %collective-permute-start.2) | collective-permute-done | bytes 49184 | tf_op jit(solution)/shard_map/while/body/eval_jaxpr/ppermute | solution.py:29
  (388 shorter events, 117.1 us)
Async XLA Ops:
  0.8 7.6 %collective-permute-start.5 = (f32[2,4,8,128]{3,2,1,0:T(8,128)S(1)}, f32[2,4,8,128]{3,2,1,0:T(8,128)S(1)}, u32[]{:S(2)}, u32[]{:S(2)}) collective-permute-start(f32[2,4,8,128]{3,2,1,0:T(8,128)S(1)} %pad_maximum_fusion.6), channel_id=1, source_target_pairs={{0,1},{1,2},{2,3},{3,4},{4,5},{5,6},{6,7},{8,9},{9,10},{10,11},{11... | collective-permute-start | bytes 98312 | tf_op jit(solution)/shard_map/ppermute | solution.py:18
  20.0 6.6 %collective-permute-start = (f32[2,3,4,8,128]{4,3,2,1,0:T(8,128)S(1)}, f32[2,3,4,8,128]{4,3,2,1,0:T(8,128)S(1)}, u32[]{:S(2)}, u32[]{:S(2)}) collective-permute-start(f32[2,3,4,8,128]{4,3,2,1,0:T(8,128)S(1)} %pad_maximum_fusion.9), channel_id=1, source_target_pairs={{1,0},{2,1},{3,2},{4,3},{5,4},{6,5},{7,6},{9,8},{10,9},{11,10},{12... | collective-permute-start | bytes 294920 | tf_op jit(solution)/shard_map/while/body/eval_jaxpr/ppermute | solution.py:21
  21.9 5.9 %collective-permute-start.1 = (f32[2,3,4,8,128]{4,3,2,1,0:T(8,128)S(1)}, f32[2,3,4,8,128]{4,3,2,1,0:T(8,128)S(1)}, u32[]{:S(2)}, u32[]{:S(2)}) collective-permute-start(f32[2,3,4,8,128]{4,3,2,1,0:T(8,128)S(1)} %pad_maximum_fusion.9), channel_id=1, source_target_pairs={{0,1},{1,2},{2,3},{3,4},{4,5},{5,6},{6,7},{8,9},{9,10},{10,11},{11... | collective-permute-start | bytes 294920 | tf_op jit(solution)/shard_map/while/body/eval_jaxpr/ppermute | solution.py:18
  28.6 6.6 %collective-permute-start = (f32[2,3,4,8,128]{4,3,2,1,0:T(8,128)S(1)}, f32[2,3,4,8,128]{4,3,2,1,0:T(8,128)S(1)}, u32[]{:S(2)}, u32[]{:S(2)}) collective-permute-start(f32[2,3,4,8,128]{4,3,2,1,0:T(8,128)S(1)} %pad_maximum_fusion.9), channel_id=1, source_target_pairs={{1,0},{2,1},{3,2},{4,3},{5,4},{6,5},{7,6},{9,8},{10,9},{11,10},{12... | collective-permute-start | bytes 294920 | tf_op jit(solution)/shard_map/while/body/eval_jaxpr/ppermute | solution.py:21
  37.3 6.6 %collective-permute-start = (f32[2,3,4,8,128]{4,3,2,1,0:T(8,128)S(1)}, f32[2,3,4,8,128]{4,3,2,1,0:T(8,128)S(1)}, u32[]{:S(2)}, u32[]{:S(2)}) collective-permute-start(f32[2,3,4,8,128]{4,3,2,1,0:T(8,128)S(1)} %pad_maximum_fusion.9), channel_id=1, source_target_pairs={{1,0},{2,1},{3,2},{4,3},{5,4},{6,5},{7,6},{9,8},{10,9},{11,10},{12... | collective-permute-start | bytes 294920 | tf_op jit(solution)/shard_map/while/body/eval_jaxpr/ppermute | solution.py:21
  39.2 5.9 %collective-permute-start.1 = (f32[2,3,4,8,128]{4,3,2,1,0:T(8,128)S(1)}, f32[2,3,4,8,128]{4,3,2,1,0:T(8,128)S(1)}, u32[]{:S(2)}, u32[]{:S(2)}) collective-permute-start(f32[2,3,4,8,128]{4,3,2,1,0:T(8,128)S(1)} %pad_maximum_fusion.9), channel_id=1, source_target_pairs={{0,1},{1,2},{2,3},{3,4},{4,5},{5,6},{6,7},{8,9},{9,10},{10,11},{11... | collective-permute-start | bytes 294920 | tf_op jit(solution)/shard_map/while/body/eval_jaxpr/ppermute | solution.py:18
  46.0 6.6 %collective-permute-start = (f32[2,3,4,8,128]{4,3,2,1,0:T(8,128)S(1)}, f32[2,3,4,8,128]{4,3,2,1,0:T(8,128)S(1)}, u32[]{:S(2)}, u32[]{:S(2)}) collective-permute-start(f32[2,3,4,8,128]{4,3,2,1,0:T(8,128)S(1)} %pad_maximum_fusion.9), channel_id=1, source_target_pairs={{1,0},{2,1},{3,2},{4,3},{5,4},{6,5},{7,6},{9,8},{10,9},{11,10},{12... | collective-permute-start | bytes 294920 | tf_op jit(solution)/shard_map/while/body/eval_jaxpr/ppermute | solution.py:21
  47.9 5.9 %collective-permute-start.1 = (f32[2,3,4,8,128]{4,3,2,1,0:T(8,128)S(1)}, f32[2,3,4,8,128]{4,3,2,1,0:T(8,128)S(1)}, u32[]{:S(2)}, u32[]{:S(2)}) collective-permute-start(f32[2,3,4,8,128]{4,3,2,1,0:T(8,128)S(1)} %pad_maximum_fusion.9), channel_id=1, source_target_pairs={{0,1},{1,2},{2,3},{3,4},{4,5},{5,6},{6,7},{8,9},{9,10},{10,11},{11... | collective-permute-start | bytes 294920 | tf_op jit(solution)/shard_map/while/body/eval_jaxpr/ppermute | solution.py:18
  54.7 6.6 %collective-permute-start = (f32[2,3,4,8,128]{4,3,2,1,0:T(8,128)S(1)}, f32[2,3,4,8,128]{4,3,2,1,0:T(8,128)S(1)}, u32[]{:S(2)}, u32[]{:S(2)}) collective-permute-start(f32[2,3,4,8,128]{4,3,2,1,0:T(8,128)S(1)} %pad_maximum_fusion.9), channel_id=1, source_target_pairs={{1,0},{2,1},{3,2},{4,3},{5,4},{6,5},{7,6},{9,8},{10,9},{11,10},{12... | collective-permute-start | bytes 294920 | tf_op jit(solution)/shard_map/while/body/eval_jaxpr/ppermute | solution.py:21
  56.6 5.9 %collective-permute-start.1 = (f32[2,3,4,8,128]{4,3,2,1,0:T(8,128)S(1)}, f32[2,3,4,8,128]{4,3,2,1,0:T(8,128)S(1)}, u32[]{:S(2)}, u32[]{:S(2)}) collective-permute-start(f32[2,3,4,8,128]{4,3,2,1,0:T(8,128)S(1)} %pad_maximum_fusion.9), channel_id=1, source_target_pairs={{0,1},{1,2},{2,3},{3,4},{4,5},{5,6},{6,7},{8,9},{9,10},{10,11},{11... | collective-permute-start | bytes 294920 | tf_op jit(solution)/shard_map/while/body/eval_jaxpr/ppermute | solution.py:18
  63.3 6.6 %collective-permute-start = (f32[2,3,4,8,128]{4,3,2,1,0:T(8,128)S(1)}, f32[2,3,4,8,128]{4,3,2,1,0:T(8,128)S(1)}, u32[]{:S(2)}, u32[]{:S(2)}) collective-permute-start(f32[2,3,4,8,128]{4,3,2,1,0:T(8,128)S(1)} %pad_maximum_fusion.9), channel_id=1, source_target_pairs={{1,0},{2,1},{3,2},{4,3},{5,4},{6,5},{7,6},{9,8},{10,9},{11,10},{12... | collective-permute-start | bytes 294920 | tf_op jit(solution)/shard_map/while/body/eval_jaxpr/ppermute | solution.py:21
  65.3 5.9 %collective-permute-start.1 = (f32[2,3,4,8,128]{4,3,2,1,0:T(8,128)S(1)}, f32[2,3,4,8,128]{4,3,2,1,0:T(8,128)S(1)}, u32[]{:S(2)}, u32[]{:S(2)}) collective-permute-start(f32[2,3,4,8,128]{4,3,2,1,0:T(8,128)S(1)} %pad_maximum_fusion.9), channel_id=1, source_target_pairs={{0,1},{1,2},{2,3},{3,4},{4,5},{5,6},{6,7},{8,9},{9,10},{10,11},{11... | collective-permute-start | bytes 294920 | tf_op jit(solution)/shard_map/while/body/eval_jaxpr/ppermute | solution.py:18
  72.0 6.6 %collective-permute-start = (f32[2,3,4,8,128]{4,3,2,1,0:T(8,128)S(1)}, f32[2,3,4,8,128]{4,3,2,1,0:T(8,128)S(1)}, u32[]{:S(2)}, u32[]{:S(2)}) collective-permute-start(f32[2,3,4,8,128]{4,3,2,1,0:T(8,128)S(1)} %pad_maximum_fusion.9), channel_id=1, source_target_pairs={{1,0},{2,1},{3,2},{4,3},{5,4},{6,5},{7,6},{9,8},{10,9},{11,10},{12... | collective-permute-start | bytes 294920 | tf_op jit(solution)/shard_map/while/body/eval_jaxpr/ppermute | solution.py:21
  80.7 6.6 %collective-permute-start = (f32[2,3,4,8,128]{4,3,2,1,0:T(8,128)S(1)}, f32[2,3,4,8,128]{4,3,2,1,0:T(8,128)S(1)}, u32[]{:S(2)}, u32[]{:S(2)}) collective-permute-start(f32[2,3,4,8,128]{4,3,2,1,0:T(8,128)S(1)} %pad_maximum_fusion.9), channel_id=1, source_target_pairs={{1,0},{2,1},{3,2},{4,3},{5,4},{6,5},{7,6},{9,8},{10,9},{11,10},{12... | collective-permute-start | bytes 294920 | tf_op jit(solution)/shard_map/while/body/eval_jaxpr/ppermute | solution.py:21
  82.6 5.9 %collective-permute-start.1 = (f32[2,3,4,8,128]{4,3,2,1,0:T(8,128)S(1)}, f32[2,3,4,8,128]{4,3,2,1,0:T(8,128)S(1)}, u32[]{:S(2)}, u32[]{:S(2)}) collective-permute-start(f32[2,3,4,8,128]{4,3,2,1,0:T(8,128)S(1)} %pad_maximum_fusion.9), channel_id=1, source_target_pairs={{0,1},{1,2},{2,3},{3,4},{4,5},{5,6},{6,7},{8,9},{9,10},{10,11},{11... | collective-permute-start | bytes 294920 | tf_op jit(solution)/shard_map/while/body/eval_jaxpr/ppermute | solution.py:18
  89.4 6.6 %collective-permute-start = (f32[2,3,4,8,128]{4,3,2,1,0:T(8,128)S(1)}, f32[2,3,4,8,128]{4,3,2,1,0:T(8,128)S(1)}, u32[]{:S(2)}, u32[]{:S(2)}) collective-permute-start(f32[2,3,4,8,128]{4,3,2,1,0:T(8,128)S(1)} %pad_maximum_fusion.9), channel_id=1, source_target_pairs={{1,0},{2,1},{3,2},{4,3},{5,4},{6,5},{7,6},{9,8},{10,9},{11,10},{12... | collective-permute-start | bytes 294920 | tf_op jit(solution)/shard_map/while/body/eval_jaxpr/ppermute | solution.py:21
  91.3 5.9 %collective-permute-start.1 = (f32[2,3,4,8,128]{4,3,2,1,0:T(8,128)S(1)}, f32[2,3,4,8,128]{4,3,2,1,0:T(8,128)S(1)}, u32[]{:S(2)}, u32[]{:S(2)}) collective-permute-start(f32[2,3,4,8,128]{4,3,2,1,0:T(8,128)S(1)} %pad_maximum_fusion.9), channel_id=1, source_target_pairs={{0,1},{1,2},{2,3},{3,4},{4,5},{5,6},{6,7},{8,9},{9,10},{10,11},{11... | collective-permute-start | bytes 294920 | tf_op jit(solution)/shard_map/while/body/eval_jaxpr/ppermute | solution.py:18
  98.0 6.6 %collective-permute-start = (f32[2,3,4,8,128]{4,3,2,1,0:T(8,128)S(1)}, f32[2,3,4,8,128]{4,3,2,1,0:T(8,128)S(1)}, u32[]{:S(2)}, u32[]{:S(2)}) collective-permute-start(f32[2,3,4,8,128]{4,3,2,1,0:T(8,128)S(1)} %pad_maximum_fusion.9), channel_id=1, source_target_pairs={{1,0},{2,1},{3,2},{4,3},{5,4},{6,5},{7,6},{9,8},{10,9},{11,10},{12... | collective-permute-start | bytes 294920 | tf_op jit(solution)/shard_map/while/body/eval_jaxpr/ppermute | solution.py:21
  100.0 5.9 %collective-permute-start.1 = (f32[2,3,4,8,128]{4,3,2,1,0:T(8,128)S(1)}, f32[2,3,4,8,128]{4,3,2,1,0:T(8,128)S(1)}, u32[]{:S(2)}, u32[]{:S(2)}) collective-permute-start(f32[2,3,4,8,128]{4,3,2,1,0:T(8,128)S(1)} %pad_maximum_fusion.9), channel_id=1, source_target_pairs={{0,1},{1,2},{2,3},{3,4},{4,5},{5,6},{6,7},{8,9},{9,10},{10,11},{11... | collective-permute-start | bytes 294920 | tf_op jit(solution)/shard_map/while/body/eval_jaxpr/ppermute | solution.py:18
  106.7 6.6 %collective-permute-start = (f32[2,3,4,8,128]{4,3,2,1,0:T(8,128)S(1)}, f32[2,3,4,8,128]{4,3,2,1,0:T(8,128)S(1)}, u32[]{:S(2)}, u32[]{:S(2)}) collective-permute-start(f32[2,3,4,8,128]{4,3,2,1,0:T(8,128)S(1)} %pad_maximum_fusion.9), channel_id=1, source_target_pairs={{1,0},{2,1},{3,2},{4,3},{5,4},{6,5},{7,6},{9,8},{10,9},{11,10},{12... | collective-permute-start | bytes 294920 | tf_op jit(solution)/shard_map/while/body/eval_jaxpr/ppermute | solution.py:21
  115.4 6.6 %collective-permute-start = (f32[2,3,4,8,128]{4,3,2,1,0:T(8,128)S(1)}, f32[2,3,4,8,128]{4,3,2,1,0:T(8,128)S(1)}, u32[]{:S(2)}, u32[]{:S(2)}) collective-permute-start(f32[2,3,4,8,128]{4,3,2,1,0:T(8,128)S(1)} %pad_maximum_fusion.9), channel_id=1, source_target_pairs={{1,0},{2,1},{3,2},{4,3},{5,4},{6,5},{7,6},{9,8},{10,9},{11,10},{12... | collective-permute-start | bytes 294920 | tf_op jit(solution)/shard_map/while/body/eval_jaxpr/ppermute | solution.py:21
  124.1 6.6 %collective-permute-start = (f32[2,3,4,8,128]{4,3,2,1,0:T(8,128)S(1)}, f32[2,3,4,8,128]{4,3,2,1,0:T(8,128)S(1)}, u32[]{:S(2)}, u32[]{:S(2)}) collective-permute-start(f32[2,3,4,8,128]{4,3,2,1,0:T(8,128)S(1)} %pad_maximum_fusion.9), channel_id=1, source_target_pairs={{1,0},{2,1},{3,2},{4,3},{5,4},{6,5},{7,6},{9,8},{10,9},{11,10},{12... | collective-permute-start | bytes 294920 | tf_op jit(solution)/shard_map/while/body/eval_jaxpr/ppermute | solution.py:21
  132.8 6.6 %collective-permute-start = (f32[2,3,4,8,128]{4,3,2,1,0:T(8,128)S(1)}, f32[2,3,4,8,128]{4,3,2,1,0:T(8,128)S(1)}, u32[]{:S(2)}, u32[]{:S(2)}) collective-permute-start(f32[2,3,4,8,128]{4,3,2,1,0:T(8,128)S(1)} %pad_maximum_fusion.9), channel_id=1, source_target_pairs={{1,0},{2,1},{3,2},{4,3},{5,4},{6,5},{7,6},{9,8},{10,9},{11,10},{12... | collective-permute-start | bytes 294920 | tf_op jit(solution)/shard_map/while/body/eval_jaxpr/ppermute | solution.py:21
  145.3 8.3 %collective-permute-start.8 = (f32[2,3,4,8,128]{4,3,2,1,0:T(8,128)S(1)}, f32[2,3,4,8,128]{4,3,2,1,0:T(8,128)S(1)}, u32[]{:S(2)}, u32[]{:S(2)}) collective-permute-start(f32[2,3,4,8,128]{4,3,2,1,0:T(8,128)S(1)} %pad_maximum_fusion.5), channel_id=1, source_target_pairs={{0,1},{1,2},{2,3},{3,4},{4,5},{5,6},{6,7},{8,9},{9,10},{10,11},{11... | collective-permute-start | bytes 294920 | tf_op jit(solution)/shard_map/ppermute | solution.py:18
  (26 other events, 127.8 us)
where the time goes:
time: 212 us; the launch traced here: 211 us
  starting transfers between devices  128 us (60%)
  waiting for transfers between devices  56.4 us (27%)
  other arithmetic  17.9 us (8%)
  local copies, waits for them, and re-layouts  6.53 us (3%)
    ppermute x21, starting transfers between devices, with_halo(): lax.ppermute(lax.slice_in_dim(block, block.shape[dim] - width, None, axis...  86.2 us
    ppermute x21, starting transfers between devices, with_halo(): lax.ppermute(lax.slice_in_dim(block, 0, width, axis=dim), axis, backward)  40.3 us
    ppermute x21, waiting for transfers between devices, with_halo(): lax.ppermute(lax.slice_in_dim(block, 0, width, axis=dim), axis, backward)  20.6 us
    ppermute x21, waiting for transfers between devices, with_halo(): lax.ppermute(lax.slice_in_dim(block, block.shape[dim] - width, None, axis...  18.9 us
    ppermute x5, waiting for transfers between devices, passed_along(): return lax.ppermute(block, axis, route)  16.9 us
    mul x60, other arithmetic, sweeps(): (driving + couple(field, faces_z, faces_x, faces_y)) / divisor * inside  10.1 us
  transfers between devices with their start and end apart: 47, of which 41 were waited for; matrix products, arithmetic and copies ran while one was open for 3% of the time, Pallas kernels for 0%

commit v1 on v0

v1 whole, which is shorter than its diff:
```python
import functools

import jax
import jax.numpy as jnp
from jax import lax
from jax.experimental import pallas as pl
from jax.experimental.pallas import tpu as pltpu
from jax.sharding import PartitionSpec as P

SWEEPS = 4
COMP = 3
LAMINATION = 8.0
MESH = pl.DeviceIdType.MESH


def respond(first, drive, coef, own):
    planes = len(drive)
    current = {SWEEPS + p: first[p] for p in range(planes)} if first is not None else None
    for _ in range(SWEEPS):
        if current is None:
            current = {SWEEPS + p: drive[p] for p in range(planes)}
            continue
        after = {}

        def add(plane, term):
            after[plane] = after[plane] + term if plane in after else term

        for plane in range(planes):
            add(SWEEPS + plane, drive[plane])
        for q, value in current.items():
            add(q + 1, coef[0, q] * value)
            add(q - 1, coef[1, q] * value)
        for q, value in current.items():
            inplane = pltpu.roll(coef[2, q] * value, 1, 0) + pltpu.roll(coef[3, q] * value, 7, 0)
            inplane2 = pltpu.roll(coef[4, q] * value, 1, 1) + pltpu.roll(
                coef[5, q] * value, coef.shape[-1] - 1, 1
            )
            add(q, inplane + inplane2)
        current = after
    return current


def kernel(
    tms,
    spaces,
    src,
    start,
    region,
    reluctivity,
    conductance,
    out,
    sent,
    landed,
    own,
    base,
    mat_own,
    mat_far,
    fine_coef,
    coarse_coef,
    cell,
    turn_sent,
    turn_landed,
    mat_ssem,
    mat_rsem,
    ssem,
    rsem,
    turn_ssem,
    turn_rsem,
):
    fine, _, planes, rows, lanes = src.shape
    tm = lax.axis_index("tm")
    me = lax.axis_index("space")
    has_left = me > 0
    has_right = me < spaces - 1
    after_tm = lax.rem(tm + 1, tms)
    before_tm = lax.rem(tm + tms - 1, tms)

    def on_side(side):
        return has_left if side == 0 else has_right

    barrier = pltpu.get_barrier_semaphore()
    for row in (after_tm, before_tm):
        pl.semaphore_signal(barrier, inc=1, device_id=(row, me), device_id_type=MESH)
    for side, step in ((0, -1), (1, 1)):

        @pl.when(on_side(side))
        def _():
            for row in (tm, after_tm, before_tm):
                pl.semaphore_signal(barrier, inc=1, device_id=(row, me + step), device_id_type=MESH)

    for p in range(planes):
        kind = region[p]
        nu = jnp.zeros((rows, lanes), jnp.float32)
        s = jnp.zeros((rows, lanes), jnp.float32)
        for level in range(reluctivity.shape[0]):
            match = kind == level
            nu = jnp.where(match, reluctivity[level], nu)
            s = jnp.where(match, conductance[level], s)
        mat_own[0, p] = nu
        mat_own[1, p] = s

    zero = jnp.zeros((rows, lanes), jnp.float32)
    for side in (0, 1):

        @pl.when(jnp.logical_not(on_side(side)))
        def _():
            mat_far[side] = jnp.zeros(mat_far.shape[1:], jnp.float32)
            turn_landed[0, 2 * side] = jnp.zeros(turn_landed.shape[2:], jnp.float32)
            turn_landed[1, 2 * side] = jnp.zeros(turn_landed.shape[2:], jnp.float32)

            def clear(slot, carry):
                landed[slot, side] = jnp.zeros(landed.shape[2:], jnp.float32)
                return carry

            lax.fori_loop(0, fine, clear, 0)

    neighbours = 2 + 3 * has_left.astype(jnp.int32) + 3 * has_right.astype(jnp.int32)
    pl.semaphore_wait(barrier, neighbours)

    def far_side(side):
        return me - 1 if side == 0 else me + 1

    def mat_copy(side):
        return pltpu.make_async_remote_copy(
            src_ref=mat_own,
            dst_ref=mat_far.at[1 - side],
            send_sem=mat_ssem.at[side],
            recv_sem=mat_rsem.at[1 - side],
            device_id=(tm, far_side(side)),
            device_id_type=MESH,
        )

    def mat_arrival(side):
        return pltpu.make_async_remote_copy(
            src_ref=mat_own,
            dst_ref=mat_far.at[side],
            send_sem=mat_ssem.at[side],
            recv_sem=mat_rsem.at[side],
            device_id=(tm, far_side(side)),
            device_id_type=MESH,
        )

    def part_copy(slot, side, c, arrival=False):
        other = side if arrival else 1 - side
        return pltpu.make_async_remote_copy(
            src_ref=sent.at[slot, side, c],
            dst_ref=landed.at[slot, other, c],
            send_sem=ssem.at[slot, side, c],
            recv_sem=rsem.at[slot, other, c],
            device_id=(tm, far_side(side)),
            device_id_type=MESH,
        )

    def turn_copy(phase, piece, c, arrival=False):
        other = piece if arrival else 2 - piece
        return pltpu.make_async_remote_copy(
            src_ref=turn_sent.at[phase, piece, c],
            dst_ref=turn_landed.at[phase, other, c],
            send_sem=turn_ssem.at[phase, piece, c],
            recv_sem=turn_rsem.at[phase, other, c],
            device_id=(after_tm, me + piece - 1),
            device_id_type=MESH,
        )

    def with_piece(piece, act):
        if piece == 1:
            act()
        else:
            pl.when(on_side(piece // 2))(act)

    for side in (0, 1):
        pl.when(on_side(side))(lambda side=side: mat_copy(side).start())
    for side in (0, 1):
        pl.when(on_side(side))(lambda side=side: mat_arrival(side).wait_recv())

    nus = [mat_far[0, 0, p] for p in range(planes)]
    nus += [mat_own[0, p] for p in range(planes)]
    nus += [mat_far[1, 0, p] for p in range(planes)]
    ss = [mat_far[0, 1, p] for p in range(planes)]
    ss += [mat_own[1, p] for p in range(planes)]
    ss += [mat_far[1, 1, p] for p in range(planes)]
    row_at = lax.broadcasted_iota(jnp.int32, (rows, lanes), 0)
    lane_at = lax.broadcasted_iota(jnp.int32, (rows, lanes), 1)
    one = jnp.float32(1.0)
    inside = [has_left.astype(jnp.float32)] * planes + [one] * planes
    inside += [has_right.astype(jnp.float32)] * planes
    for q in range(1, 3 * planes - 1):
        nu, s = nus[q], ss[q]
        up_z = (0.5 * LAMINATION) * (nus[q + 1] + nu)
        down_z = (0.5 * LAMINATION) * (nus[q - 1] + nu)
        up_x = 0.5 * (nu + jnp.where(row_at < rows - 1, pltpu.roll(nu, rows - 1, 0), 0.0))
        down_x = 0.5 * (nu + jnp.where(row_at > 0, pltpu.roll(nu, 1, 0), 0.0))
        up_y = 0.5 * (nu + jnp.where(lane_at < lanes - 1, pltpu.roll(nu, lanes - 1, 1), 0.0))
        down_y = 0.5 * (nu + jnp.where(lane_at > 0, pltpu.roll(nu, 1, 1), 0.0))
        summed = up_z + down_z + up_x + down_x + up_y + down_y
        gives = [
            up_z,
            down_z,
            jnp.where(row_at < rows - 1, up_x, 0.0),
            jnp.where(row_at > 0, down_x, 0.0),
            jnp.where(lane_at < lanes - 1, up_y, 0.0),
            jnp.where(lane_at > 0, down_y, 0.0),
        ]
        outside = 1.0 - inside[q]
        fine_d = s + summed
        coarse_d = s / fine + summed
        fine_inv = inside[q] / (fine_d + outside)
        coarse_inv = inside[q] / (coarse_d + outside)
        for which in range(6):
            fine_coef[which, q] = gives[which] * fine_inv
            coarse_coef[which, q] = gives[which] * coarse_inv
        if planes <= q < 2 * planes:
            p = q - planes
            cell[0, p] = fine_inv
            cell[1, p] = s * fine_inv
            cell[2, p] = fine_d
            cell[3, p] = coarse_inv
            cell[4, p] = s / fine * coarse_inv
            cell[5, p] = coarse_d

    def spread(reach, slot, c):
        for p in range(planes):
            sent[slot, 0, c, p] = reach[p] if p in reach else zero
            sent[slot, 1, c, p] = reach[2 * planes + p] if 2 * planes + p in reach else zero
        for side in (0, 1):
            pl.when(on_side(side))(lambda side=side: part_copy(slot, side, c).start())

    def gathered(slot, c):
        for side in (0, 1):
            pl.when(on_side(side))(lambda side=side: part_copy(slot, side, c, True).wait_recv())
        return [landed[slot, 0, c, p] + landed[slot, 1, c, p] for p in range(planes)]

    def turn_spread(reach, phase, c):
        for piece in range(3):
            for p in range(planes):
                turn_sent[phase, piece, c, p] = reach[piece * planes + p]
        for piece in range(3):
            with_piece(piece, lambda piece=piece: turn_copy(phase, piece, c).start())

    def turn_gathered(phase, c):
        for piece in range(3):
            with_piece(piece, lambda piece=piece: turn_copy(phase, piece, c, True).wait_recv())
        return [
            turn_landed[phase, 0, c, p] + turn_landed[phase, 1, c, p] + turn_landed[phase, 2, c, p]
            for p in range(planes)
        ]

    for c in range(COMP):
        first = [cell[2, p] * start[0, c, p] for p in range(planes)]
        drive = [cell[1, p] * first[p] + src[1, c, p] for p in range(planes)]
        reach = respond(first, drive, fine_coef, own)
        spread(reach, 1, c)
        for p in range(planes):
            own[c, p] = reach[planes + p]

    for c in range(COMP):
        reach = respond(None, [src[0, c, p] for p in range(planes)], fine_coef, own)
        spread(reach, 0, c)
        for p in range(planes):
            base[c, p] = reach[planes + p] - cell[2, p] * start[0, c, p]

    def one_step(j, carry):
        for c in range(COMP):
            arrived = gathered(j - 1, c)
            first = [own[c, p] + arrived[p] for p in range(planes)]
            drive = [cell[1, p] * first[p] + src[j, c, p] for p in range(planes)]
            reach = respond(first, drive, fine_coef, own)
            spread(reach, j, c)
            for p in range(planes):
                own[c, p] = reach[planes + p]
                out[j - 1, c, p] = first[p] * cell[0, p]
        return carry

    lax.fori_loop(2, fine, one_step, 0)

    for c in range(COMP):
        arrived = gathered(fine - 1, c)
        first = [own[c, p] + arrived[p] for p in range(planes)]
        drive = [cell[1, p] * first[p] for p in range(planes)]
        turn_spread(respond(first, drive, fine_coef, own), 0, c)
        for p in range(planes):
            out[fine - 1, c, p] = first[p] * cell[0, p]

    for c in range(COMP):
        arrived = gathered(0, c)
        for p in range(planes):
            base[c, p] = base[c, p] + arrived[p]

    last = tm == tms - 1
    for c in range(COMP):
        arrived = turn_gathered(0, c)
        for p in range(planes):
            base[c, p] = (base[c, p] + arrived[p]) * cell[0, p] * cell[5, p]

        @pl.when(last)
        def _():
            first = [base[c, p] for p in range(planes)]
            drive = [cell[4, p] * first[p] for p in range(planes)]
            turn_spread(respond(first, drive, coarse_coef, own), 1, c)

    for c in range(COMP):
        arrived = turn_gathered(1, c)
        for p in range(planes):
            base[c, p] = base[c, p] + arrived[p]

        @pl.when(jnp.logical_not(last))
        def _():
            first = [base[c, p] for p in range(planes)]
            drive = [cell[4, p] * first[p] for p in range(planes)]
            turn_spread(respond(first, drive, coarse_coef, own), 1, c)

        for p in range(planes):
            out[0, c, p] = start[0, c, p] + base[c, p] * cell[3, p]

    for side in (0, 1):

        @pl.when(on_side(side))
        def _():
            mat_copy(side).wait_send()

            def left(slot, carry):
                for c in range(COMP):
                    part_copy(slot, side, c).wait_send()
                return carry

            lax.fori_loop(0, fine, left, 0)

    for phase in (0, 1):
        for piece in range(3):
            for c in range(COMP):
                with_piece(piece, lambda: turn_copy(phase, piece, c).wait_send())


def local(source, coarse_start, region, reluctivity, conductance):
    fine, comp, planes, rows, lanes = source.shape
    vmem = pl.BlockSpec(memory_space=pltpu.VMEM)
    smem = pl.BlockSpec(memory_space=pltpu.SMEM)
    slab = (planes, rows, lanes)
    return pl.pallas_call(
        functools.partial(kernel, lax.axis_size("tm"), lax.axis_size("space")),
        out_shape=jax.ShapeDtypeStruct(source.shape, source.dtype),
        in_specs=[vmem, vmem, vmem, smem, smem],
        out_specs=vmem,
        scratch_shapes=[
            pltpu.VMEM((fine, 2, comp) + slab, jnp.float32),
            pltpu.VMEM((fine, 2, comp) + slab, jnp.float32),
            pltpu.VMEM((comp,) + slab, jnp.float32),
            pltpu.VMEM((comp,) + slab, jnp.float32),
            pltpu.VMEM((2,) + slab, jnp.float32),
            pltpu.VMEM((2, 2) + slab, jnp.float32),
            pltpu.VMEM((6, 3 * planes, rows, lanes), jnp.float32),
            pltpu.VMEM((6, 3 * planes, rows, lanes), jnp.float32),
            pltpu.VMEM((6,) + slab, jnp.float32),
            pltpu.VMEM((2, 3, comp) + slab, jnp.float32),
            pltpu.VMEM((2, 3, comp) + slab, jnp.float32),
            pltpu.SemaphoreType.DMA((2,)),
            pltpu.SemaphoreType.DMA((2,)),
            pltpu.SemaphoreType.DMA((fine, 2, comp)),
            pltpu.SemaphoreType.DMA((fine, 2, comp)),
            pltpu.SemaphoreType.DMA((2, 3, comp)),
            pltpu.SemaphoreType.DMA((2, 3, comp)),
        ],
        compiler_params=pltpu.CompilerParams(
            collective_id=0, has_side_effects=True, vmem_limit_bytes=32 * 1024 * 1024
        ),
        cost_estimate=pl.CostEstimate(
            flops=20_000_000, bytes_accessed=1_800_000, transcendentals=0
        ),
    )(source, coarse_start, region, reluctivity, conductance)


def solution(mesh):
    placed = (
        P("tm", None, "space", None, None),
        P("tm", None, "space", None, None),
        P("space", None, None),
        P(),
        P(),
    )
    return jax.shard_map(
        local,
        mesh=mesh,
        in_specs=placed,
        out_specs=P("tm", None, "space", None, None),
        check_vma=False,
    )
```

time: 212 us -> 72.3 us (0.34)
  the two profiles are of different devices: /device:TPU:1 before, /device:TPU:15 now
where the time goes in v1:
time: 72.3 us; the launch traced here: 72 us
  Pallas kernels  67.1 us (93%)
  local copies, waits for them, and re-layouts  4.84 us (7%)
    pallas_call x1, Pallas kernels, local(): pl.pallas_call(functools.partial(kernel, lax.axis_size('tm'), lax.axis_si...  67.1 us
    unnamed x11, local copies, waits for them, and re-layouts  4.84 us

profile of v1, /device:TPU:15, one launch (start us, length us, event | category | flops | bytes accessed | tf_op | source)
XLA Modules:
  0.0 72.0 jit_solution(4333413385068648962)
XLA Ops:
  0.0 0.0 copy-start
  0.0 1.1 %copy-done = f32[16,3,4,8,128]{4,3,2,1,0:T(8,128)S(1)} copy-done((f32[16,3,4,8,128]{4,3,2,1,0:T(8,128)S(1)}, f32[16,3,4,8,128]{4,3,2,1,0:T(8,128)}, u32[]{:S(2)}) %copy-start) | copy-done | bytes 786456
  1.1 0.0 copy-start.1
  1.1 0.8 %copy-done.1 = f32[1,3,4,8,128]{4,3,2,1,0:T(8,128)S(1)} copy-done((f32[1,3,4,8,128]{4,3,2,1,0:T(8,128)S(1)}, f32[1,3,4,8,128]{4,3,2,1,0:T(8,128)}, u32[]{:S(2)}) %copy-start.1) | copy-done | bytes 49176
  1.9 0.0 copy-start.2
  1.9 0.7 copy-done.2
  2.7 0.0 copy-start.3
  2.7 0.7 copy-done.3
  3.3 0.0 copy-start.4
  3.3 0.7 copy-done.4
  4.0 67.1 %shard_map.55 = f32[16,3,4,8,128]{4,3,2,1,0:T(8,128)S(1)} custom-call(f32[16,3,4,8,128]{4,3,2,1,0:T(8,128)S(1)} %copy-done, f32[1,3,4,8,128]{4,3,2,1,0:T(8,128)S(1)} %copy-done.1, s32[4,8,128]{2,1,0:T(8,128)S(1)} %copy-done.2, f32[8]{0:T(128)S(1)} %copy-done.3, f32[8]{0:T(128)S(1)} %copy-done.4), custom_call_target="tpu_custom_call" | custom-call | flops 20000000 | bytes 1800000 | tf_op jit(solution)/shard_map/pallas_call | solution.py:339
  71.1 0.9 %copy.7 = f32[16,3,4,8,128]{4,3,2,1,0:T(8,128)} copy(f32[16,3,4,8,128]{4,3,2,1,0:T(8,128)S(1)} %shard_map.55) | data formatting | bytes 1572864
Async XLA Ops:
  0.0 1.1 %copy-start = (f32[16,3,4,8,128]{4,3,2,1,0:T(8,128)S(1)}, f32[16,3,4,8,128]{4,3,2,1,0:T(8,128)}, u32[]{:S(2)}) copy-start(f32[16,3,4,8,128]{4,3,2,1,0:T(8,128)} %src.1) | copy-start | bytes 2359300
  1.1 0.8 %copy-start.1 = (f32[1,3,4,8,128]{4,3,2,1,0:T(8,128)S(1)}, f32[1,3,4,8,128]{4,3,2,1,0:T(8,128)}, u32[]{:S(2)}) copy-start(f32[1,3,4,8,128]{4,3,2,1,0:T(8,128)} %start.1) | copy-start | bytes 147460
  1.9 0.7 copy-start.2
  2.7 0.7 copy-start.3
  3.3 0.7 copy-start.4

commit v2 on v1

v2 whole, which is shorter than its diff:
```python
import functools

import jax
import jax.numpy as jnp
from jax import lax
from jax.experimental import pallas as pl
from jax.experimental.pallas import tpu as pltpu
from jax.sharding import PartitionSpec as P

SWEEPS = 4
COMP = 3
LAMINATION = 8.0
SHIFTS = (-2, -1, 1, 2)
MESH = pl.DeviceIdType.MESH


def respond(first, drive, coef):
    current = first
    for _ in range(SWEEPS):
        if current is None:
            current = dict(drive)
            continue
        after = dict(drive)

        def add(plane, term):
            after[plane] = after[plane] + term if plane in after else term

        for q, value in current.items():
            add(q + 1, coef[0, q] * value)
            add(q - 1, coef[1, q] * value)
        for q, value in current.items():
            in_x = pltpu.roll(coef[2, q] * value, 1, 0) + pltpu.roll(coef[3, q] * value, 7, 0)
            in_y = pltpu.roll(coef[4, q] * value, 1, 1) + pltpu.roll(
                coef[5, q] * value, coef.shape[-1] - 1, 1
            )
            add(q, in_x + in_y)
        current = after
    return current


def kernel(
    tms,
    spaces,
    src,
    start,
    region,
    reluctivity,
    conductance,
    out,
    sent,
    landed,
    own,
    base,
    mat_own,
    mat_far,
    fine_coef,
    coarse_coef,
    pull,
    cell,
    turn_sent,
    turn_landed,
    mat_ssem,
    mat_rsem,
    ssem,
    rsem,
    turn_ssem,
    turn_rsem,
):
    fine, _, planes, rows, lanes = src.shape
    tm = lax.axis_index("tm")
    me = lax.axis_index("space")
    after_tm = lax.rem(tm + 1, tms)
    before_tm = lax.rem(tm + tms - 1, tms)
    mid = 2 * planes

    def reaches(shift):
        return me + shift >= 0 if shift < 0 else me + shift < spaces

    barrier = pltpu.get_barrier_semaphore()
    for row in (after_tm, before_tm):
        pl.semaphore_signal(barrier, inc=1, device_id=(row, me), device_id_type=MESH)
    neighbours = jnp.int32(2)
    for shift in SHIFTS:
        neighbours = neighbours + 3 * reaches(shift).astype(jnp.int32)

        @pl.when(reaches(shift))
        def _():
            for row in (tm, after_tm, before_tm):
                pl.semaphore_signal(barrier, inc=1, device_id=(row, me + shift), device_id_type=MESH)

    for p in range(planes):
        kind = region[p]
        nu = jnp.zeros((rows, lanes), jnp.float32)
        s = jnp.zeros((rows, lanes), jnp.float32)
        for level in range(reluctivity.shape[0]):
            match = kind == level
            nu = jnp.where(match, reluctivity[level], nu)
            s = jnp.where(match, conductance[level], s)
        mat_own[0, p] = nu
        mat_own[1, p] = s

    zero = jnp.zeros((rows, lanes), jnp.float32)
    for at, shift in enumerate(SHIFTS):

        @pl.when(jnp.logical_not(reaches(shift)))
        def _():
            mat_far[at] = jnp.zeros(mat_far.shape[1:], jnp.float32)
            for phase in (0, 1):
                turn_landed[phase, 2 + shift] = jnp.zeros(turn_landed.shape[2:], jnp.float32)

            def clear(slot, carry):
                landed[slot, at] = jnp.zeros(landed.shape[2:], jnp.float32)
                return carry

            lax.fori_loop(0, fine, clear, 0)

    pl.semaphore_wait(barrier, neighbours)

    def mat_copy(at, arrival=False):
        other = at if arrival else 3 - at
        return pltpu.make_async_remote_copy(
            src_ref=mat_own,
            dst_ref=mat_far.at[other],
            send_sem=mat_ssem.at[at],
            recv_sem=mat_rsem.at[other],
            device_id=(tm, me + SHIFTS[at]),
            device_id_type=MESH,
        )

    def part_copy(slot, at, c, arrival=False):
        other = at if arrival else 3 - at
        return pltpu.make_async_remote_copy(
            src_ref=sent.at[slot, at, c],
            dst_ref=landed.at[slot, other, c],
            send_sem=ssem.at[slot, at, c],
            recv_sem=rsem.at[slot, other, c],
            device_id=(tm, me + SHIFTS[at]),
            device_id_type=MESH,
        )

    def turn_copy(phase, piece, c, arrival=False):
        other = piece if arrival else 4 - piece
        return pltpu.make_async_remote_copy(
            src_ref=turn_sent.at[phase, piece, c],
            dst_ref=turn_landed.at[phase, other, c],
            send_sem=turn_ssem.at[phase, piece, c],
            recv_sem=turn_rsem.at[phase, other, c],
            device_id=(after_tm, me + piece - 2),
            device_id_type=MESH,
        )

    def with_piece(piece, act):
        if piece == 2:
            act()
        else:
            pl.when(reaches(piece - 2))(act)

    for at in (1, 2, 0, 3):
        pl.when(reaches(SHIFTS[at]))(lambda at=at: mat_copy(at).start())
    for at in (1, 2, 0, 3):
        pl.when(reaches(SHIFTS[at]))(lambda at=at: mat_copy(at, True).wait_recv())

    def whole(kind):
        gathered_planes = []
        for at in (0, 1, None, 2, 3):
            for p in range(planes):
                gathered_planes.append(mat_own[kind, p] if at is None else mat_far[at, kind, p])
        return gathered_planes

    nus, ss = whole(0), whole(1)
    row_at = lax.broadcasted_iota(jnp.int32, (rows, lanes), 0)
    lane_at = lax.broadcasted_iota(jnp.int32, (rows, lanes), 1)
    inside = []
    for shift in (-2, -1, 0, 1, 2):
        held = reaches(shift).astype(jnp.float32) if shift else jnp.float32(1.0)
        inside += [held] * planes
    for q in range(1, 5 * planes - 1):
        nu, s = nus[q], ss[q]
        up_z = (0.5 * LAMINATION) * (nus[q + 1] + nu)
        down_z = (0.5 * LAMINATION) * (nus[q - 1] + nu)
        up_x = 0.5 * (nu + jnp.where(row_at < rows - 1, pltpu.roll(nu, rows - 1, 0), 0.0))
        down_x = 0.5 * (nu + jnp.where(row_at > 0, pltpu.roll(nu, 1, 0), 0.0))
        up_y = 0.5 * (nu + jnp.where(lane_at < lanes - 1, pltpu.roll(nu, lanes - 1, 1), 0.0))
        down_y = 0.5 * (nu + jnp.where(lane_at > 0, pltpu.roll(nu, 1, 1), 0.0))
        summed = up_z + down_z + up_x + down_x + up_y + down_y
        gives = [
            up_z,
            down_z,
            jnp.where(row_at < rows - 1, up_x, 0.0),
            jnp.where(row_at > 0, down_x, 0.0),
            jnp.where(lane_at < lanes - 1, up_y, 0.0),
            jnp.where(lane_at > 0, down_y, 0.0),
        ]
        outside = 1.0 - inside[q]
        fine_d = s + summed
        coarse_d = s / fine + summed
        fine_inv = inside[q] / (fine_d + outside)
        coarse_inv = inside[q] / (coarse_d + outside)
        pull[q] = s * fine_inv
        for which in range(6):
            fine_coef[which, q] = gives[which] * fine_inv
            if planes < q < 4 * planes - 1:
                coarse_coef[which, q] = gives[which] * coarse_inv
        if mid <= q < mid + planes:
            p = q - mid
            cell[0, p] = fine_inv
            cell[2, p] = fine_d
            cell[3, p] = coarse_inv
            cell[4, p] = s / fine * coarse_inv
            cell[5, p] = coarse_d

    def store(reach, slot, at, c):
        begin = mid + SHIFTS[at] * planes
        for p in range(planes):
            sent[slot, at, c, p] = reach[begin + p] if begin + p in reach else zero

    def ship(slot, at, c):
        pl.when(reaches(SHIFTS[at]))(lambda: part_copy(slot, at, c).start())

    def gathered(slot, c, sides):
        for at in sides:
            pl.when(reaches(SHIFTS[at]))(lambda at=at: part_copy(slot, at, c, True).wait_recv())
        total = []
        for p in range(planes):
            value = landed[slot, sides[0], c, p]
            for at in sides[1:]:
                value = value + landed[slot, at, c, p]
            total.append(value)
        return total

    def turn_spread(reach, phase, c, pieces):
        for piece in pieces:
            for p in range(planes):
                turn_sent[phase, piece, c, p] = reach[piece * planes + p]
        for piece in pieces:
            with_piece(piece, lambda piece=piece: turn_copy(phase, piece, c).start())

    def turn_gathered(phase, c, pieces):
        for piece in pieces:
            with_piece(piece, lambda piece=piece: turn_copy(phase, piece, c, True).wait_recv())
        total = []
        for p in range(planes):
            value = turn_landed[phase, pieces[0], c, p]
            for piece in pieces[1:]:
                value = value + turn_landed[phase, piece, c, p]
            total.append(value)
        return total

    near, every = (1, 2), (0, 1, 2, 3)
    span = range(planes)

    def fine_drive(state, slot, c):
        drive = {q: pull[q] * value for q, value in state.items()}
        if slot is not None:
            for p in span:
                drive[mid + p] = drive[mid + p] + src[slot, c, p]
        return drive

    def two_steps(values, slot, c, final=False):
        state = {mid + p: values[p] for p in span}
        halfway = respond(state, fine_drive(state, slot, c), fine_coef)
        reach = respond(
            halfway, fine_drive(halfway, None if final else slot + 1, c), fine_coef
        )
        for at in near:
            store(halfway, slot, at, c)
        if final:
            turn_spread(reach, 0, c, range(5))
        else:
            for at in every:
                store(reach, slot + 1, at, c)
            for at in every:
                ship(slot + 1, at, c)
            for p in span:
                own[c, p] = reach[mid + p]
        for at in near:
            ship(slot, at, c)
        for p in span:
            out[slot, c, p] = halfway[mid + p]

    for c in range(COMP):
        two_steps([cell[2, p] * start[0, c, p] for p in span], 1, c)

    for c in range(COMP):
        reach = respond(None, {mid + p: src[0, c, p] for p in span}, fine_coef)
        for at in near:
            store(reach, 0, at, c)
        for at in near:
            ship(0, at, c)
        for p in span:
            base[c, p] = reach[mid + p] - cell[2, p] * start[0, c, p]

    def arrive(slot, c):
        arrived = gathered(slot, c, every)
        values = [own[c, p] + arrived[p] for p in span]
        for p in span:
            out[slot, c, p] = values[p] * cell[0, p]
        return values

    def one_pair(pair, carry):
        for c in range(COMP):
            two_steps(arrive(2 * pair, c), 2 * pair + 1, c)
        return carry

    lax.fori_loop(1, fine // 2 - 1, one_pair, 0)
    for c in range(COMP):
        two_steps(arrive(fine - 2, c), fine - 1, c, True)

    def finish(slot):
        for c in range(COMP):
            arrived = gathered(slot, c, near)
            for p in span:
                out[slot, c, p] = (out[slot, c, p] + arrived[p]) * cell[0, p]

    for c in range(COMP):
        arrived = gathered(0, c, near)
        for p in span:
            base[c, p] = base[c, p] + arrived[p]

    def finish_pair(pair, carry):
        finish(2 * pair + 1)
        return carry

    lax.fori_loop(0, fine // 2 - 1, finish_pair, 0)

    last = tm == tms - 1
    inner = (1, 2, 3)

    def coarse_turn(c):
        first = {mid + p: base[c, p] for p in span}
        drive = {mid + p: cell[4, p] * base[c, p] for p in span}
        turn_spread(respond(first, drive, coarse_coef), 1, c, inner)

    for c in range(COMP):
        arrived = turn_gathered(0, c, range(5))
        for p in span:
            base[c, p] = (base[c, p] + arrived[p]) * cell[0, p] * cell[5, p]
        pl.when(last)(lambda c=c: coarse_turn(c))

    for c in range(COMP):
        arrived = turn_gathered(1, c, inner)
        for p in span:
            base[c, p] = base[c, p] + arrived[p]
        pl.when(jnp.logical_not(last))(lambda c=c: coarse_turn(c))
        for p in span:
            out[0, c, p] = start[0, c, p] + base[c, p] * cell[3, p]
    finish(fine - 1)

    for at in every:

        @pl.when(reaches(SHIFTS[at]))
        def _():
            mat_copy(at).wait_send()

            def left(slot, carry):
                for c in range(COMP):
                    part_copy(slot if at in near else 2 * slot, at, c).wait_send()
                return carry

            if at in near:
                lax.fori_loop(0, fine, left, 0)
            else:
                lax.fori_loop(1, fine // 2, left, 0)

    for phase in (0, 1):
        for piece in range(5) if phase == 0 else inner:
            for c in range(COMP):
                with_piece(piece, lambda: turn_copy(phase, piece, c).wait_send())


def local(source, coarse_start, region, reluctivity, conductance):
    fine, comp, planes, rows, lanes = source.shape
    vmem = pl.BlockSpec(memory_space=pltpu.VMEM)
    smem = pl.BlockSpec(memory_space=pltpu.SMEM)
    slab = (planes, rows, lanes)
    return pl.pallas_call(
        functools.partial(kernel, lax.axis_size("tm"), lax.axis_size("space")),
        out_shape=jax.ShapeDtypeStruct(source.shape, source.dtype),
        in_specs=[vmem, vmem, vmem, smem, smem],
        out_specs=vmem,
        scratch_shapes=[
            pltpu.VMEM((fine, 4, comp) + slab, jnp.float32),
            pltpu.VMEM((fine, 4, comp) + slab, jnp.float32),
            pltpu.VMEM((comp,) + slab, jnp.float32),
            pltpu.VMEM((comp,) + slab, jnp.float32),
            pltpu.VMEM((2,) + slab, jnp.float32),
            pltpu.VMEM((4, 2) + slab, jnp.float32),
            pltpu.VMEM((6, 5 * planes, rows, lanes), jnp.float32),
            pltpu.VMEM((6, 5 * planes, rows, lanes), jnp.float32),
            pltpu.VMEM((5 * planes, rows, lanes), jnp.float32),
            pltpu.VMEM((6,) + slab, jnp.float32),
            pltpu.VMEM((2, 5, comp) + slab, jnp.float32),
            pltpu.VMEM((2, 5, comp) + slab, jnp.float32),
            pltpu.SemaphoreType.DMA((4,)),
            pltpu.SemaphoreType.DMA((4,)),
            pltpu.SemaphoreType.DMA((fine, 4, comp)),
            pltpu.SemaphoreType.DMA((fine, 4, comp)),
            pltpu.SemaphoreType.DMA((2, 5, comp)),
            pltpu.SemaphoreType.DMA((2, 5, comp)),
        ],
        compiler_params=pltpu.CompilerParams(
            collective_id=0, has_side_effects=True, vmem_limit_bytes=32 * 1024 * 1024
        ),
        cost_estimate=pl.CostEstimate(
            flops=20_000_000, bytes_accessed=1_800_000, transcendentals=0
        ),
    )(source, coarse_start, region, reluctivity, conductance)


def solution(mesh):
    placed = (
        P("tm", None, "space", None, None),
        P("tm", None, "space", None, None),
        P("space", None, None),
        P(),
        P(),
    )
    return jax.shard_map(
        local,
        mesh=mesh,
        in_specs=placed,
        out_specs=P("tm", None, "space", None, None),
        check_vma=False,
    )
```

time: 72.3 us -> 63.6 us (0.88)
  Pallas kernels: 67.1 us -> 58.5 us
    pallas_call x1, Pallas kernels: 67.1 us -> 58.5 us  [local(): pl.pallas_call(functools.partial(kernel, lax.axis_size('tm'), lax.axis_si...]
where the time goes in v2:
time: 63.6 us; the launch traced here: 63.3 us
  Pallas kernels  58.5 us (92%)
  local copies, waits for them, and re-layouts  4.84 us (8%)
    pallas_call x1, Pallas kernels, local(): pl.pallas_call(functools.partial(kernel, lax.axis_size('tm'), lax.axis_si...  58.5 us
    unnamed x11, local copies, waits for them, and re-layouts  4.84 us

profile of v2, /device:TPU:15, one launch (start us, length us, event | category | flops | bytes accessed | tf_op | source)
XLA Modules:
  0.0 63.3 jit_solution(14100182711422672402)
XLA Ops:
  0.0 0.0 copy-start
  0.0 1.1 %copy-done = f32[16,3,4,8,128]{4,3,2,1,0:T(8,128)S(1)} copy-done((f32[16,3,4,8,128]{4,3,2,1,0:T(8,128)S(1)}, f32[16,3,4,8,128]{4,3,2,1,0:T(8,128)}, u32[]{:S(2)}) %copy-start) | copy-done | bytes 786456
  1.1 0.0 copy-start.1
  1.1 0.8 %copy-done.1 = f32[1,3,4,8,128]{4,3,2,1,0:T(8,128)S(1)} copy-done((f32[1,3,4,8,128]{4,3,2,1,0:T(8,128)S(1)}, f32[1,3,4,8,128]{4,3,2,1,0:T(8,128)}, u32[]{:S(2)}) %copy-start.1) | copy-done | bytes 49176
  1.9 0.0 copy-start.2
  1.9 0.7 %copy-done.2 = s32[4,8,128]{2,1,0:T(8,128)S(1)} copy-done((s32[4,8,128]{2,1,0:T(8,128)S(1)}, s32[4,8,128]{2,1,0:T(8,128)}, u32[]{:S(2)}) %copy-start.2) | copy-done | bytes 16408
  2.7 0.0 copy-start.3
  2.7 0.7 %copy-done.3 = f32[8]{0:T(128)S(1)} copy-done((f32[8]{0:T(128)S(1)}, f32[8]{0:T(128)}, u32[]{:S(2)}) %copy-start.3) | copy-done | bytes 56
  3.3 0.0 copy-start.4
  3.3 0.7 %copy-done.4 = f32[8]{0:T(128)S(1)} copy-done((f32[8]{0:T(128)S(1)}, f32[8]{0:T(128)}, u32[]{:S(2)}) %copy-start.4) | copy-done | bytes 56
  4.0 58.5 %shard_map.55 = f32[16,3,4,8,128]{4,3,2,1,0:T(8,128)S(1)} custom-call(f32[16,3,4,8,128]{4,3,2,1,0:T(8,128)S(1)} %copy-done, f32[1,3,4,8,128]{4,3,2,1,0:T(8,128)S(1)} %copy-done.1, s32[4,8,128]{2,1,0:T(8,128)S(1)} %copy-done.2, f32[8]{0:T(128)S(1)} %copy-done.3, f32[8]{0:T(128)S(1)} %copy-done.4), custom_call_target="tpu_custom_call" | custom-call | flops 20000000 | bytes 1800000 | tf_op jit(solution)/shard_map/pallas_call | solution.py:376
  62.4 0.9 %copy.7 = f32[16,3,4,8,128]{4,3,2,1,0:T(8,128)} copy(f32[16,3,4,8,128]{4,3,2,1,0:T(8,128)S(1)} %shard_map.55) | data formatting | bytes 1572864
Async XLA Ops:
  0.0 1.1 %copy-start = (f32[16,3,4,8,128]{4,3,2,1,0:T(8,128)S(1)}, f32[16,3,4,8,128]{4,3,2,1,0:T(8,128)}, u32[]{:S(2)}) copy-start(f32[16,3,4,8,128]{4,3,2,1,0:T(8,128)} %src.1) | copy-start | bytes 2359300
  1.1 0.8 %copy-start.1 = (f32[1,3,4,8,128]{4,3,2,1,0:T(8,128)S(1)}, f32[1,3,4,8,128]{4,3,2,1,0:T(8,128)}, u32[]{:S(2)}) copy-start(f32[1,3,4,8,128]{4,3,2,1,0:T(8,128)} %start.1) | copy-start | bytes 147460
  1.9 0.7 %copy-start.2 = (s32[4,8,128]{2,1,0:T(8,128)S(1)}, s32[4,8,128]{2,1,0:T(8,128)}, u32[]{:S(2)}) copy-start(s32[4,8,128]{2,1,0:T(8,128)} %region.1) | copy-start | bytes 49156
  2.7 0.7 %copy-start.3 = (f32[8]{0:T(128)S(1)}, f32[8]{0:T(128)}, u32[]{:S(2)}) copy-start(f32[8]{0:T(128)} %reluctivity.1) | copy-start | bytes 100
  3.3 0.7 %copy-start.4 = (f32[8]{0:T(128)S(1)}, f32[8]{0:T(128)}, u32[]{:S(2)}) copy-start(f32[8]{0:T(128)} %conductance.1) | copy-start | bytes 100

commit v3 on v2

--- a/solution.py
+++ b/solution.py
@@ -41,12 +41,18 @@
 def kernel(
     tms,
     spaces,
+    src_in,
+    start_in,
+    region_in,
+    reluctivity_in,
+    conductance_in,
+    out,
     src,
     start,
     region,
     reluctivity,
     conductance,
-    out,
+    in_sem,
     sent,
     landed,
     own,
@@ -56,6 +62,7 @@
     fine_coef,
     coarse_coef,
     pull,
+    coarse_pull,
     cell,
     turn_sent,
     turn_landed,
@@ -67,27 +74,46 @@
     turn_rsem,
 ):
     fine, _, planes, rows, lanes = src.shape
+    loads = [
+        pltpu.make_async_copy(held, kept, in_sem.at[i])
+        for i, (held, kept) in enumerate(
+            (
+                (reluctivity_in, reluctivity),
+                (conductance_in, conductance),
+                (region_in, region),
+                (start_in, start),
+                (src_in, src),
+            )
+        )
+    ]
+    for load in loads:
+        load.start()
     tm = lax.axis_index("tm")
     me = lax.axis_index("space")
     after_tm = lax.rem(tm + 1, tms)
     before_tm = lax.rem(tm + tms - 1, tms)
+    after_two = lax.rem(tm + 2, tms)
+    before_two = lax.rem(tm + tms - 2, tms)
     mid = 2 * planes
 
     def reaches(shift):
         return me + shift >= 0 if shift < 0 else me + shift < spaces
 
     barrier = pltpu.get_barrier_semaphore()
-    for row in (after_tm, before_tm):
+    others = (after_tm, before_tm, after_two, before_two)
+    for row in others:
         pl.semaphore_signal(barrier, inc=1, device_id=(row, me), device_id_type=MESH)
-    neighbours = jnp.int32(2)
+    neighbours = jnp.int32(4)
     for shift in SHIFTS:
-        neighbours = neighbours + 3 * reaches(shift).astype(jnp.int32)
+        neighbours = neighbours + 5 * reaches(shift).astype(jnp.int32)
 
         @pl.when(reaches(shift))
         def _():
-            for row in (tm, after_tm, before_tm):
+            for row in (tm,) + others:
                 pl.semaphore_signal(barrier, inc=1, device_id=(row, me + shift), device_id_type=MESH)
 
+    for load in loads[:3]:
+        load.wait()
     for p in range(planes):
         kind = region[p]
         nu = jnp.zeros((rows, lanes), jnp.float32)
@@ -105,7 +131,7 @@
         @pl.when(jnp.logical_not(reaches(shift)))
         def _():
             mat_far[at] = jnp.zeros(mat_far.shape[1:], jnp.float32)
-            for phase in (0, 1):
+            for phase in (0, 1, 2):
                 turn_landed[phase, 2 + shift] = jnp.zeros(turn_landed.shape[2:], jnp.float32)
 
             def clear(slot, carry):
@@ -127,6 +153,17 @@
             device_id_type=MESH,
         )
 
+    def whole_copy(slot, at, arrival=False):
+        other = at if arrival else 3 - at
+        return pltpu.make_async_remote_copy(
+            src_ref=sent.at[slot, at],
+            dst_ref=landed.at[slot, other],
+            send_sem=ssem.at[slot, at, 0],
+            recv_sem=rsem.at[slot, other, 0],
+            device_id=(tm, me + SHIFTS[at]),
+            device_id_type=MESH,
+        )
+
     def part_copy(slot, at, c, arrival=False):
         other = at if arrival else 3 - at
         return pltpu.make_async_remote_copy(
@@ -145,7 +182,7 @@
             dst_ref=turn_landed.at[phase, other, c],
             send_sem=turn_ssem.at[phase, piece, c],
             recv_sem=turn_rsem.at[phase, other, c],
-            device_id=(after_tm, me + piece - 2),
+            device_id=(after_two if phase == 2 else after_tm, me + piece - 2),
             device_id_type=MESH,
         )
 
@@ -157,6 +194,8 @@
 
     for at in (1, 2, 0, 3):
         pl.when(reaches(SHIFTS[at]))(lambda at=at: mat_copy(at).start())
+    for load in loads[3:]:
+        load.wait()
     for at in (1, 2, 0, 3):
         pl.when(reaches(SHIFTS[at]))(lambda at=at: mat_copy(at, True).wait_recv())
 
@@ -197,16 +236,15 @@
         fine_inv = inside[q] / (fine_d + outside)
         coarse_inv = inside[q] / (coarse_d + outside)
         pull[q] = s * fine_inv
+        coarse_pull[q] = s / fine * coarse_inv
         for which in range(6):
             fine_coef[which, q] = gives[which] * fine_inv
-            if planes < q < 4 * planes - 1:
-                coarse_coef[which, q] = gives[which] * coarse_inv
+            coarse_coef[which, q] = gives[which] * coarse_inv
         if mid <= q < mid + planes:
             p = q - mid
             cell[0, p] = fine_inv
             cell[2, p] = fine_d
             cell[3, p] = coarse_inv
-            cell[4, p] = s / fine * coarse_inv
             cell[5, p] = coarse_d
 
     def store(reach, slot, at, c):
@@ -217,9 +255,20 @@
     def ship(slot, at, c):
         pl.when(reaches(SHIFTS[at]))(lambda: part_copy(slot, at, c).start())
 
+    def ship_whole(slot):
+        for at in near:
+            pl.when(reaches(SHIFTS[at]))(lambda at=at: whole_copy(slot, at).start())
+
+    def await_whole(slot):
+        for at in near:
+            pl.when(reaches(SHIFTS[at]))(lambda at=at: whole_copy(slot, at, True).wait_recv())
+
     def gathered(slot, c, sides):
         for at in sides:
             pl.when(reaches(SHIFTS[at]))(lambda at=at: part_copy(slot, at, c, True).wait_recv())
+        return landed_sum(slot, c, sides)
+
+    def landed_sum(slot, c, sides):
         total = []
         for p in range(planes):
             value = landed[slot, sides[0], c, p]
@@ -273,22 +322,20 @@
                 ship(slot + 1, at, c)
             for p in span:
                 own[c, p] = reach[mid + p]
-        for at in near:
-            ship(slot, at, c)
         for p in span:
             out[slot, c, p] = halfway[mid + p]
 
     for c in range(COMP):
         two_steps([cell[2, p] * start[0, c, p] for p in span], 1, c)
+    ship_whole(1)
 
     for c in range(COMP):
         reach = respond(None, {mid + p: src[0, c, p] for p in span}, fine_coef)
         for at in near:
             store(reach, 0, at, c)
-        for at in near:
-            ship(0, at, c)
         for p in span:
             base[c, p] = reach[mid + p] - cell[2, p] * start[0, c, p]
+    ship_whole(0)
 
     def arrive(slot, c):
         arrived = gathered(slot, c, every)
@@ -300,20 +347,24 @@
     def one_pair(pair, carry):
         for c in range(COMP):
             two_steps(arrive(2 * pair, c), 2 * pair + 1, c)
+        ship_whole(2 * pair + 1)
         return carry
 
     lax.fori_loop(1, fine // 2 - 1, one_pair, 0)
     for c in range(COMP):
         two_steps(arrive(fine - 2, c), fine - 1, c, True)
+    ship_whole(fine - 1)
 
     def finish(slot):
+        await_whole(slot)
         for c in range(COMP):
-            arrived = gathered(slot, c, near)
+            arrived = landed_sum(slot, c, near)
             for p in span:
                 out[slot, c, p] = (out[slot, c, p] + arrived[p]) * cell[0, p]
 
+    await_whole(0)
     for c in range(COMP):
-        arrived = gathered(0, c, near)
+        arrived = landed_sum(0, c, near)
         for p in span:
             base[c, p] = base[c, p] + arrived[p]
 
@@ -324,24 +375,34 @@
     lax.fori_loop(0, fine // 2 - 1, finish_pair, 0)
 
     last = tm == tms - 1
+    odd = lax.rem(tm, 2) == 1
     inner = (1, 2, 3)
 
-    def coarse_turn(c):
-        first = {mid + p: base[c, p] for p in span}
-        drive = {mid + p: cell[4, p] * base[c, p] for p in span}
-        turn_spread(respond(first, drive, coarse_coef), 1, c, inner)
+    def one_turn(state):
+        return respond(state, {q: coarse_pull[q] * v for q, v in state.items()}, coarse_coef)
+
+    def give(c, both):
+        once = one_turn({mid + p: base[c, p] for p in span})
+        turn_spread(once, 1, c, inner)
+        if both:
+            turn_spread(one_turn(once), 2, c, range(5))
+
+    def take(phase, c, pieces):
+        arrived = turn_gathered(phase, c, pieces)
+        for p in span:
+            base[c, p] = base[c, p] + arrived[p]
 
     for c in range(COMP):
-        arrived = turn_gathered(0, c, range(5))
-        for p in span:
-            base[c, p] = (base[c, p] + arrived[p]) * cell[0, p] * cell[5, p]
-        pl.when(last)(lambda c=c: coarse_turn(c))
+        take(0, c, range(5))
+        for p in span:
+            base[c, p] = base[c, p] * cell[0, p] * cell[5, p]
+        pl.when(jnp.logical_not(odd))(lambda c=c: give(c, False))
+        pl.when(last)(lambda c=c: give(c, True))
 
     for c in range(COMP):
-        arrived = turn_gathered(1, c, inner)
-        for p in span:
-            base[c, p] = base[c, p] + arrived[p]
-        pl.when(jnp.logical_not(last))(lambda c=c: coarse_turn(c))
+        take(1, c, inner)
+        pl.when(odd)(lambda c=c: take(2, c, range(5)))
+        pl.when(jnp.logical_and(odd, jnp.logical_not(last)))(lambda c=c: give(c, True))
         for p in span:
             out[0, c, p] = start[0, c, p] + base[c, p] * cell[3, p]
     finish(fine - 1)
@@ -352,33 +413,48 @@
         def _():
             mat_copy(at).wait_send()
 
-            def left(slot, carry):
+            def left(pair, carry):
                 for c in range(COMP):
-                    part_copy(slot if at in near else 2 * slot, at, c).wait_send()
+                    part_copy(2 * pair, at, c).wait_send()
                 return carry
 
+            lax.fori_loop(1, fine // 2, left, 0)
             if at in near:
-                lax.fori_loop(0, fine, left, 0)
-            else:
-                lax.fori_loop(1, fine // 2, left, 0)
-
-    for phase in (0, 1):
-        for piece in range(5) if phase == 0 else inner:
+
+                def left_whole(pair, carry):
+                    whole_copy(2 * pair + 1, at).wait_send()
+                    return carry
+
+                lax.fori_loop(0, fine // 2, left_whole, 0)
+                whole_copy(0, at).wait_send()
+
+    def turns_left(phase, pieces):
+        for piece in pieces:
             for c in range(COMP):
                 with_piece(piece, lambda: turn_copy(phase, piece, c).wait_send())
+
+    turns_left(0, range(5))
+    turns_left(1, inner)
+    pl.when(odd)(lambda: turns_left(2, range(5)))
 
 
 def local(source, coarse_start, region, reluctivity, conductance):
     fine, comp, planes, rows, lanes = source.shape
     vmem = pl.BlockSpec(memory_space=pltpu.VMEM)
-    smem = pl.BlockSpec(memory_space=pltpu.SMEM)
+    hbm = pl.BlockSpec(memory_space=pltpu.HBM)
     slab = (planes, rows, lanes)
     return pl.pallas_call(
         functools.partial(kernel, lax.axis_size("tm"), lax.axis_size("space")),
         out_shape=jax.ShapeDtypeStruct(source.shape, source.dtype),
-        in_specs=[vmem, vmem, vmem, smem, smem],
+        in_specs=[hbm] * 5,
         out_specs=vmem,
         scratch_shapes=[
+            pltpu.VMEM(source.shape, jnp.float32),
+            pltpu.VMEM(coarse_start.shape, jnp.float32),
+            pltpu.VMEM(region.shape, jnp.int32),
+            pltpu.SMEM(reluctivity.shape, jnp.float32),
+            pltpu.SMEM(conductance.shape, jnp.float32),
+            pltpu.SemaphoreType.DMA((5,)),
             pltpu.VMEM((fine, 4, comp) + slab, jnp.float32),
             pltpu.VMEM((fine, 4, comp) + slab, jnp.float32),
             pltpu.VMEM((comp,) + slab, jnp.float32),
@@ -388,15 +464,16 @@
             pltpu.VMEM((6, 5 * planes, rows, lanes), jnp.float32),
             pltpu.VMEM((6, 5 * planes, rows, lanes), jnp.float32),
             pltpu.VMEM((5 * planes, rows, lanes), jnp.float32),
+            pltpu.VMEM((5 * planes, rows, lanes), jnp.float32),
             pltpu.VMEM((6,) + slab, jnp.float32),
-            pltpu.VMEM((2, 5, comp) + slab, jnp.float32),
-            pltpu.VMEM((2, 5, comp) + slab, jnp.float32),
+            pltpu.VMEM((3, 5, comp) + slab, jnp.float32),
+            pltpu.VMEM((3, 5, comp) + slab, jnp.float32),
             pltpu.SemaphoreType.DMA((4,)),
             pltpu.SemaphoreType.DMA((4,)),
             pltpu.SemaphoreType.DMA((fine, 4, comp)),
             pltpu.SemaphoreType.DMA((fine, 4, comp)),
-            pltpu.SemaphoreType.DMA((2, 5, comp)),
-            pltpu.SemaphoreType.DMA((2, 5, comp)),
+            pltpu.SemaphoreType.DMA((3, 5, comp)),
+            pltpu.SemaphoreType.DMA((3, 5, comp)),
         ],
         compiler_params=pltpu.CompilerParams(
             collective_id=0, has_side_effects=True, vmem_limit_bytes=32 * 1024 * 1024

time: 63.6 us -> 57.9 us (0.910)
  Pallas kernels: 58.5 us -> 52.8 us
    pallas_call x1, Pallas kernels: 58.5 us -> 52.8 us  [local(): pl.pallas_call(functools.partial(kernel, lax.axis_size('tm'), lax.axis_si...]
where the time goes in v3:
time: 57.9 us; the launch traced here: 57.6 us
  Pallas kernels  52.8 us (91%)
  local copies, waits for them, and re-layouts  4.84 us (8%)
    pallas_call x1, Pallas kernels, local(): pl.pallas_call(functools.partial(kernel, lax.axis_size('tm'), lax.axis_si...  52.8 us
    unnamed x11, local copies, waits for them, and re-layouts  4.84 us

profile of v3, /device:TPU:15, one launch (start us, length us, event | category | flops | bytes accessed | tf_op | source)
XLA Modules:
  0.0 57.6 jit_solution(12990463447783636275)
XLA Ops:
  0.0 0.0 copy-start
  0.0 1.1 %copy-done = f32[16,3,4,8,128]{4,3,2,1,0:T(8,128)S(1)} copy-done((f32[16,3,4,8,128]{4,3,2,1,0:T(8,128)S(1)}, f32[16,3,4,8,128]{4,3,2,1,0:T(8,128)}, u32[]{:S(2)}) %copy-start) | copy-done | bytes 786456
  1.1 0.0 copy-start.1
  1.1 0.8 %copy-done.1 = f32[1,3,4,8,128]{4,3,2,1,0:T(8,128)S(1)} copy-done((f32[1,3,4,8,128]{4,3,2,1,0:T(8,128)S(1)}, f32[1,3,4,8,128]{4,3,2,1,0:T(8,128)}, u32[]{:S(2)}) %copy-start.1) | copy-done | bytes 49176
  1.9 0.0 copy-start.2
  1.9 0.7 %copy-done.2 = s32[4,8,128]{2,1,0:T(8,128)S(1)} copy-done((s32[4,8,128]{2,1,0:T(8,128)S(1)}, s32[4,8,128]{2,1,0:T(8,128)}, u32[]{:S(2)}) %copy-start.2) | copy-done | bytes 16408
  2.7 0.0 copy-start.3
  2.7 0.7 %copy-done.3 = f32[8]{0:T(128)S(1)} copy-done((f32[8]{0:T(128)S(1)}, f32[8]{0:T(128)}, u32[]{:S(2)}) %copy-start.3) | copy-done | bytes 56
  3.3 0.0 copy-start.4
  3.3 0.7 %copy-done.4 = f32[8]{0:T(128)S(1)} copy-done((f32[8]{0:T(128)S(1)}, f32[8]{0:T(128)}, u32[]{:S(2)}) %copy-start.4) | copy-done | bytes 56
  4.0 52.8 %shard_map.55 = f32[16,3,4,8,128]{4,3,2,1,0:T(8,128)S(1)} custom-call(f32[16,3,4,8,128]{4,3,2,1,0:T(8,128)S(1)} %copy-done, f32[1,3,4,8,128]{4,3,2,1,0:T(8,128)S(1)} %copy-done.1, s32[4,8,128]{2,1,0:T(8,128)S(1)} %copy-done.2, f32[8]{0:T(128)S(1)} %copy-done.3, f32[8]{0:T(128)S(1)} %copy-done.4), custom_call_target="tpu_custom_call" | custom-call | flops 20000000 | bytes 1800000 | tf_op jit(solution)/shard_map/pallas_call | solution.py:446
  56.8 0.9 %copy.7 = f32[16,3,4,8,128]{4,3,2,1,0:T(8,128)} copy(f32[16,3,4,8,128]{4,3,2,1,0:T(8,128)S(1)} %shard_map.55) | data formatting | bytes 1572864
Async XLA Ops:
  0.0 1.1 %copy-start = (f32[16,3,4,8,128]{4,3,2,1,0:T(8,128)S(1)}, f32[16,3,4,8,128]{4,3,2,1,0:T(8,128)}, u32[]{:S(2)}) copy-start(f32[16,3,4,8,128]{4,3,2,1,0:T(8,128)} %src_in.1) | copy-start | bytes 2359300
  1.1 0.8 %copy-start.1 = (f32[1,3,4,8,128]{4,3,2,1,0:T(8,128)S(1)}, f32[1,3,4,8,128]{4,3,2,1,0:T(8,128)}, u32[]{:S(2)}) copy-start(f32[1,3,4,8,128]{4,3,2,1,0:T(8,128)} %start_in.1) | copy-start | bytes 147460
  1.9 0.7 %copy-start.2 = (s32[4,8,128]{2,1,0:T(8,128)S(1)}, s32[4,8,128]{2,1,0:T(8,128)}, u32[]{:S(2)}) copy-start(s32[4,8,128]{2,1,0:T(8,128)} %region_in.1) | copy-start | bytes 49156
  2.7 0.7 %copy-start.3 = (f32[8]{0:T(128)S(1)}, f32[8]{0:T(128)}, u32[]{:S(2)}) copy-start(f32[8]{0:T(128)} %reluctivity_in.1) | copy-start | bytes 100
  3.3 0.7 %copy-start.4 = (f32[8]{0:T(128)S(1)}, f32[8]{0:T(128)}, u32[]{:S(2)}) copy-start(f32[8]{0:T(128)} %conductance_in.1) | copy-start | bytes 100

commit v4 on v3

--- a/solution.py
+++ b/solution.py
@@ -374,6 +374,27 @@
 
     lax.fori_loop(0, fine // 2 - 1, finish_pair, 0)
 
+    for at in every:
+
+        @pl.when(reaches(SHIFTS[at]))
+        def _():
+            mat_copy(at).wait_send()
+
+            def left(pair, carry):
+                for c in range(COMP):
+                    part_copy(2 * pair, at, c).wait_send()
+                return carry
+
+            lax.fori_loop(1, fine // 2, left, 0)
+            if at in near:
+
+                def left_whole(pair, carry):
+                    whole_copy(2 * pair + 1, at).wait_send()
+                    return carry
+
+                lax.fori_loop(0, fine // 2 - 1, left_whole, 0)
+                whole_copy(0, at).wait_send()
+
     last = tm == tms - 1
     odd = lax.rem(tm, 2) == 1
     inner = (1, 2, 3)
@@ -407,26 +428,8 @@
             out[0, c, p] = start[0, c, p] + base[c, p] * cell[3, p]
     finish(fine - 1)
 
-    for at in every:
-
-        @pl.when(reaches(SHIFTS[at]))
-        def _():
-            mat_copy(at).wait_send()
-
-            def left(pair, carry):
-                for c in range(COMP):
-                    part_copy(2 * pair, at, c).wait_send()
-                return carry
-
-            lax.fori_loop(1, fine // 2, left, 0)
-            if at in near:
-
-                def left_whole(pair, carry):
-                    whole_copy(2 * pair + 1, at).wait_send()
-                    return carry
-
-                lax.fori_loop(0, fine // 2, left_whole, 0)
-                whole_copy(0, at).wait_send()
+    for at in near:
+        pl.when(reaches(SHIFTS[at]))(lambda at=at: whole_copy(fine - 1, at).wait_send())
 
     def turns_left(phase, pieces):
         for piece in pieces:

time: 57.9 us -> 57.5 us (level)
  no operation moved by 1% of the time
where the time goes in v4:
time: 57.5 us; the launch traced here: 57.2 us
  Pallas kernels  52.4 us (91%)
  local copies, waits for them, and re-layouts  4.84 us (8%)
    pallas_call x1, Pallas kernels, local(): pl.pallas_call(functools.partial(kernel, lax.axis_size('tm'), lax.axis_si...  52.4 us
    unnamed x11, local copies, waits for them, and re-layouts  4.84 us

profile of v4, /device:TPU:15, one launch (start us, length us, event | category | flops | bytes accessed | tf_op | source)
XLA Modules:
  0.0 57.2 jit_solution(8867160424818174588)
XLA Ops:
  0.0 0.0 copy-start
  0.0 1.1 %copy-done = f32[16,3,4,8,128]{4,3,2,1,0:T(8,128)S(1)} copy-done((f32[16,3,4,8,128]{4,3,2,1,0:T(8,128)S(1)}, f32[16,3,4,8,128]{4,3,2,1,0:T(8,128)}, u32[]{:S(2)}) %copy-start) | copy-done | bytes 786456
  1.1 0.0 copy-start.1
  1.1 0.8 %copy-done.1 = f32[1,3,4,8,128]{4,3,2,1,0:T(8,128)S(1)} copy-done((f32[1,3,4,8,128]{4,3,2,1,0:T(8,128)S(1)}, f32[1,3,4,8,128]{4,3,2,1,0:T(8,128)}, u32[]{:S(2)}) %copy-start.1) | copy-done | bytes 49176
  1.9 0.0 copy-start.2
  1.9 0.7 %copy-done.2 = s32[4,8,128]{2,1,0:T(8,128)S(1)} copy-done((s32[4,8,128]{2,1,0:T(8,128)S(1)}, s32[4,8,128]{2,1,0:T(8,128)}, u32[]{:S(2)}) %copy-start.2) | copy-done | bytes 16408
  2.7 0.0 copy-start.3
  2.7 0.7 %copy-done.3 = f32[8]{0:T(128)S(1)} copy-done((f32[8]{0:T(128)S(1)}, f32[8]{0:T(128)}, u32[]{:S(2)}) %copy-start.3) | copy-done | bytes 56
  3.3 0.0 copy-start.4
  3.3 0.7 %copy-done.4 = f32[8]{0:T(128)S(1)} copy-done((f32[8]{0:T(128)S(1)}, f32[8]{0:T(128)}, u32[]{:S(2)}) %copy-start.4) | copy-done | bytes 56
  4.0 52.4 %shard_map.55 = f32[16,3,4,8,128]{4,3,2,1,0:T(8,128)S(1)} custom-call(f32[16,3,4,8,128]{4,3,2,1,0:T(8,128)S(1)} %copy-done, f32[1,3,4,8,128]{4,3,2,1,0:T(8,128)S(1)} %copy-done.1, s32[4,8,128]{2,1,0:T(8,128)S(1)} %copy-done.2, f32[8]{0:T(128)S(1)} %copy-done.3, f32[8]{0:T(128)S(1)} %copy-done.4), custom_call_target="tpu_custom_call" | custom-call | flops 20000000 | bytes 1800000 | tf_op jit(solution)/shard_map/pallas_call | solution.py:449
  56.4 0.9 %copy.7 = f32[16,3,4,8,128]{4,3,2,1,0:T(8,128)} copy(f32[16,3,4,8,128]{4,3,2,1,0:T(8,128)S(1)} %shard_map.55) | data formatting | bytes 1572864
Async XLA Ops:
  0.0 1.1 %copy-start = (f32[16,3,4,8,128]{4,3,2,1,0:T(8,128)S(1)}, f32[16,3,4,8,128]{4,3,2,1,0:T(8,128)}, u32[]{:S(2)}) copy-start(f32[16,3,4,8,128]{4,3,2,1,0:T(8,128)} %src_in.1) | copy-start | bytes 2359300
  1.1 0.8 %copy-start.1 = (f32[1,3,4,8,128]{4,3,2,1,0:T(8,128)S(1)}, f32[1,3,4,8,128]{4,3,2,1,0:T(8,128)}, u32[]{:S(2)}) copy-start(f32[1,3,4,8,128]{4,3,2,1,0:T(8,128)} %start_in.1) | copy-start | bytes 147460
  1.9 0.7 %copy-start.2 = (s32[4,8,128]{2,1,0:T(8,128)S(1)}, s32[4,8,128]{2,1,0:T(8,128)}, u32[]{:S(2)}) copy-start(s32[4,8,128]{2,1,0:T(8,128)} %region_in.1) | copy-start | bytes 49156
  2.7 0.7 %copy-start.3 = (f32[8]{0:T(128)S(1)}, f32[8]{0:T(128)}, u32[]{:S(2)}) copy-start(f32[8]{0:T(128)} %reluctivity_in.1) | copy-start | bytes 100
  3.3 0.7 %copy-start.4 = (f32[8]{0:T(128)S(1)}, f32[8]{0:T(128)}, u32[]{:S(2)}) copy-start(f32[8]{0:T(128)} %conductance_in.1) | copy-start | bytes 100
